TPU v7x, 256 devices: a whole 4x4x8 slice. The times are simulated.
256 devices in a mesh: dp: 64 (over x, y, z_hi, core), tp: 4 (over z_lo).
Axes of the slice: x: 4, y: 4, z: 8 (z_hi: 2, z_lo: 4; z = z_hi * 4 + z_lo), core: 2. Of those that a mesh axis runs over, the one named last changes fastest.
Arguments:
- queries: bfloat16 [384, 128, 576], P('dp', 'tp'), may hold values from -100 to 100
- latent_cache: bfloat16 [384, 320, 576], P('dp'), may hold values from -5 to 5
- lengths: int32 [384], P('dp'), may hold values from 2 to 320, as said below
- slot_row: int32 [384], replicated, may hold values from 0 to 383, each once
- w_uv: bfloat16 [128, 512, 128], P('tp'), may hold values from -0.25 to 0.25
- w_o: bfloat16 [16384, 7168], P('tp', 'dp'), may hold values from -0.046875 to 0.046875
- resid: bfloat16 [384, 7168], P(None, 'dp'), may hold values from -3 to 3
- norm_gain: bfloat16 [7168], replicated, may hold values from 0.099609375 to 1.8984375
- w_gate: bfloat16 [7168, 18432], P('tp', 'dp'), may hold values from -0.0625 to 0.0625
- w_up: bfloat16 [7168, 18432], P('tp', 'dp'), may hold values from -0.0625 to 0.0625
- w_down: bfloat16 [18432, 7168], P('dp', 'tp'), may hold values from -0.046875 to 0.046875
Outputs:
- layer_out: bfloat16 [384, 7168], P('dp', 'tp')
Inputs may be any that keep to these rules, and one draw needn't show every extreme that they name: `lengths`: each row's live length; every row has at least positions 0 and 1 live, and some row reaches 320.
All inputs are finite; a program needn't handle non-finite values.
Results may differ from a plain program's by a relative error of at most 0.02.
Values may be sent and summed in bfloat16 or wider, within the bound.
A program may use at most 64 MiB of HBM per device.

v0:
```python
import jax
import jax.numpy as jnp
from jax import lax
from jax.sharding import PartitionSpec as P

softmax_scale = 192.0 ** (-0.5)


def normalize(hidden_state, norm_gain):
    wide = hidden_state.astype(jnp.float32)
    scale_rows = lax.rsqrt(jnp.mean(wide * wide, axis=1, keepdims=True) + 1e-06)
    return (wide * scale_rows * norm_gain.astype(jnp.float32)).astype(jnp.bfloat16)


def on_device(
    queries, latent_cache, lengths, slot_row, w_uv, w_o, resid, norm_gain, w_gate, w_up, w_down
):
    rows_here = queries.shape[0]
    latent_width = w_uv.shape[1]
    scores = (
        jnp.einsum("rhk,rpk->rhp", queries, latent_cache, preferred_element_type=jnp.float32)
        * softmax_scale
    )
    positions = lax.broadcasted_iota(jnp.int32, scores.shape, 2)
    live = positions < lengths[:, None, None]
    top = jnp.max(jnp.where(live, scores, -1e30), axis=2, keepdims=True)
    weights = jnp.where(live, jnp.exp(scores - top), 0.0)
    probs = (weights / jnp.sum(weights, axis=2, keepdims=True)).astype(jnp.bfloat16)
    latent_out = jnp.einsum(
        "rhp,rpk->rhk", probs, latent_cache[:, :, :latent_width], preferred_element_type=jnp.float32
    ).astype(jnp.bfloat16)
    values = jnp.einsum("rhk,hkd->rhd", latent_out, w_uv, preferred_element_type=jnp.float32)
    values = values.astype(jnp.bfloat16).reshape(rows_here, -1)
    partial_value = jnp.dot(
        lax.all_gather(values, "dp", axis=0, tiled=True), w_o, preferred_element_type=jnp.float32
    )
    attention = lax.psum(partial_value, "tp")
    total_rows = slot_row.shape[0]
    inverse = (
        jnp.zeros((total_rows,), jnp.int32)
        .at[slot_row]
        .set(jnp.arange(total_rows, dtype=jnp.int32))
    )
    hidden_block = (resid.astype(jnp.float32) + attention[inverse]).astype(jnp.bfloat16)
    tp_place = lax.axis_index("tp")
    col_width = w_gate.shape[0]
    full_state = lax.all_gather(hidden_block, "dp", axis=1, tiled=True)
    normed_full = normalize(full_state, norm_gain)
    normed = lax.dynamic_slice_in_dim(normed_full, tp_place * col_width, col_width, 1)
    state_cols = lax.dynamic_slice_in_dim(full_state, tp_place * col_width, col_width, 1)
    gate = jnp.dot(normed, w_gate, preferred_element_type=jnp.float32)
    up = jnp.dot(normed, w_up, preferred_element_type=jnp.float32)
    stacked = jnp.concatenate([gate, up], axis=1)
    hidden_width = w_gate.shape[1]
    summed = lax.psum(stacked.astype(jnp.bfloat16), "tp").astype(jnp.float32)
    activated = (jax.nn.silu(summed[:, :hidden_width]) * summed[:, hidden_width:]).astype(
        jnp.bfloat16
    )
    down = lax.psum_scatter(
        jnp.dot(activated, w_down, preferred_element_type=jnp.float32),
        "dp",
        scatter_dimension=0,
        tiled=True,
    )
    dp_place = lax.axis_index("dp")
    state_mine = lax.dynamic_slice_in_dim(state_cols, dp_place * rows_here, rows_here, 0)
    return (state_mine.astype(jnp.float32) + down).astype(jnp.bfloat16)


def solution(mesh):
    placed = (
        P("dp", "tp", None),
        P("dp", None, None),
        P("dp"),
        P(),
        P("tp", None, None),
        P("tp", "dp"),
        P(None, "dp"),
        P(),
        P("tp", "dp"),
        P("tp", "dp"),
        P("dp", "tp"),
    )
    return jax.shard_map(
        on_device, mesh=mesh, in_specs=placed, out_specs=P("dp", "tp"), check_vma=False
    )
```

profile of v0, /device:TPU:32, one launch (start us, length us, event | category | flops | bytes accessed | tf_op | source)
XLA Modules:
  0.0 619.8 jit_solution(13371777728480265894)
XLA Ops:
  6.5 2.7 convolution_multiply_fusion
  10.4 2.4 fusion.6
  12.8 3.6 fusion.12
  16.5 2.9 scatter_custom_fusion
  19.4 91.7 %all-gather.6.cloned.1.call-done = bf16[64,6,4096]{2,1,0:T(8,128)(2,1)} async-done(((bf16[1,6,4096]{2,1,0:T(8,128)(2,1)}), bf16[64,6,4096]{2,1,0:T(8,128)(2,1)}) %all-gather.6.cloned.1.call-update) | async-done | bytes 3145744 | tf_op jit(solution)/shard_map/all_gather | solution.py:35
  111.2 5.7 reshape.35
  116.9 3.7 fusion.38
  120.6 41.5 %all-reduce.5.cloned.1.call-done = f32[384,112]{0,1:T(8,128)} async-done(((f32[384,112]{0,1:T(8,128)}), f32[384,112]{0,1:T(8,128)}) %all-reduce.5.cloned.1.call-update) | async-done | bytes 172048 | tf_op jit(solution)/shard_map/psum | solution.py:37
  163.2 1.1 gather_fusion
  165.3 99.2 %all-gather.4.cloned.1.call-done = bf16[384,7168]{0,1:T(8,128)(2,1)} async-done(((bf16[384,112]{0,1:T(8,128)(2,1)}), bf16[384,7168]{0,1:T(8,128)(2,1)}) %all-gather.4.cloned.1.call-update) | async-done | bytes 5505040 | tf_op jit(solution)/shard_map/all_gather | solution.py:47
  264.5 4.0 multiply_reduce_fusion
  272.8 43.8 %all-reduce.7.cloned.1.call-done = bf16[384,576]{0,1:T(8,128)(2,1)} async-done(((bf16[384,576]{0,1:T(8,128)(2,1)}), bf16[384,576]{0,1:T(8,128)(2,1)}) %all-reduce.7.cloned.1.call-update) | async-done | bytes 442384 | tf_op jit(solution)/shard_map/psum | solution.py:55
  317.6 2.5 fusion.16
  320.1 234.1 %fusion = f32[8,1792]{1,0:T(8,128)S(1)} fusion(f32[384,1792]{1,0:T(8,128)} %fusion.16), kind=kCustom, calls=%all-reduce-scatter | all-reduce-scatter fusion | flops 917505 | bytes 2810880
  554.3 1.3 collective-permute-start.15
  555.6 1.3 collective-permute-start.14
  556.9 1.3 collective-permute-start.13
  558.2 1.3 collective-permute-start.12
  559.5 1.3 collective-permute-start.11
  560.8 1.3 collective-permute-start.10
  562.1 18.7 %collective-permute-start.9 = (f32[8,1792]{1,0:T(8,128)S(1)}, f32[8,1792]{1,0:T(8,128)S(1)}, u32[]{:S(2)}, u32[]{:S(2)}) collective-permute-start(f32[8,1792]{1,0:T(8,128)S(1)} %fusion), channel_id=1, source_target_pairs={{0,40},{4,44},{8,48},{12,52},{16,56},{20,60},{24,64},{28,68},{32,7... | collective-permute-start | bytes 172040
  580.8 1.3 collective-permute-start.8
  582.1 1.3 collective-permute-start.7
  583.4 3.8 collective-permute-start.6
  587.2 3.1 collective-permute-start.5
  590.4 2.2 collective-permute-start.4
  592.6 2.2 collective-permute-start.3
  594.7 8.8 %collective-permute-start.2 = (f32[8,1792]{1,0:T(8,128)S(1)}, f32[8,1792]{1,0:T(8,128)S(1)}, u32[]{:S(2)}, u32[]{:S(2)}) collective-permute-start(f32[8,1792]{1,0:T(8,128)S(1)} %fusion), channel_id=1, source_target_pairs={{0,12},{4,16},{8,20},{12,24},{16,28},{20,32},{24,36},{28,40},{32,4... | collective-permute-start | bytes 172040
  603.6 2.2 collective-permute-start.1
  605.8 1.7 collective-permute-start
  608.8 1.5 dynamic_slice.7
  610.6 2.0 concatenate.5
  (67 shorter events, 10.0 us)
Async XLA Ops:
  6.5 311.1 %copy-start = (bf16[288,1792]{1,0:T(8,128)(2,1)S(1)}, bf16[288,1792]{1,0:T(8,128)(2,1)}, u32[]{:S(2)}) copy-start(bf16[288,1792]{1,0:T(8,128)(2,1)} %param.21) | copy-start | bytes 3096580
  6.5 3.8 copy-start.2
  6.5 3.5 copy-start.11
  6.5 104.6 %all-gather.6.cloned.1.call-start = ((), (), s32[]{:S(2)}) async-start(), calls=%async_computation.3 | async-start | bytes 4259840 | tf_op jit(solution)/shard_map/all_gather | solution.py:35
  9.3 0.7 copy-start.4
  12.8 3.7 copy-start.7
  16.4 145.7 %all-reduce.5.cloned.1.call-start = ((), (), s32[]{:S(2)}) async-start(), calls=%async_computation | async-start | bytes 344064 | tf_op jit(solution)/shard_map/psum | solution.py:37
  19.4 97.4 %copy-start.3 = (bf16[4096,112]{0,1:T(8,128)(2,1)S(1)}, bf16[4096,112]{0,1:T(8,128)(2,1)}, u32[]{:S(2)}) copy-start(bf16[4096,112]{0,1:T(8,128)(2,1)} %param.16) | copy-start | bytes 2752516
  116.9 47.6 %copy-start.5 = (bf16[384,112]{0,1:T(8,128)(2,1)S(1)}, bf16[384,112]{0,1:T(8,128)(2,1)}, u32[]{:S(2)}) copy-start(bf16[384,112]{0,1:T(8,128)(2,1)} %param.17) | copy-start | bytes 258052
  116.9 48.3 %copy-start.6 = (bf16[7168]{0:T(1024)(128)(2,1)S(1)}, bf16[7168]{0:T(1024)(128)(2,1)}, u32[]{:S(2)}) copy-start(bf16[7168]{0:T(1024)(128)(2,1)} %param.18) | copy-start | bytes 43012
  120.6 143.9 %all-gather.4.cloned.1.call-start = ((), (), s32[]{:S(2)}) async-start(), calls=%async_computation.1 | async-start | bytes 5591040 | tf_op jit(solution)/shard_map/all_gather | solution.py:47
  165.1 151.4 %all-reduce.7.cloned.1.call-start = ((), (), s32[]{:S(2)}) async-start(), calls=%async_computation.2 | async-start | bytes 884736 | tf_op jit(solution)/shard_map/psum | solution.py:55
  264.5 4.2 copy-start.1
  268.7 1.2 copy-start.9
  269.9 1.2 copy-start.10
  317.6 290.0 %copy-start.8 = (u32[256]{0:T(256)S(1)}, u32[256]{0:T(256)}, u32[]{:S(2)}) copy-start(u32[256]{0:T(256)} %constant.59) | copy-start | bytes 3076
  554.3 6.5 %collective-permute-start.15 = (f32[6,1792]{1,0:T(8,128)S(1)}, f32[6,1792]{1,0:T(8,128)S(1)}, u32[]{:S(2)}, u32[]{:S(2)}) collective-permute-start(f32[6,1792]{1,0:T(8,128)S(1)} %slice.16), channel_id=1, source_target_pairs={{0,64},{4,68},{8,72},{12,76},{16,80},{20,84},{24,88},{28,92},{32,9... | collective-permute-start | bytes 129032
  555.6 6.5 %collective-permute-start.14 = (f32[8,1792]{1,0:T(8,128)S(1)}, f32[8,1792]{1,0:T(8,128)S(1)}, u32[]{:S(2)}, u32[]{:S(2)}) collective-permute-start(f32[8,1792]{1,0:T(8,128)S(1)} %fusion), channel_id=1, source_target_pairs={{0,60},{4,64},{8,68},{12,72},{16,76},{20,80},{24,84},{28,88},{32,9... | collective-permute-start | bytes 172040
  556.9 23.9 %collective-permute-start.13 = (f32[8,1792]{1,0:T(8,128)S(1)}, f32[8,1792]{1,0:T(8,128)S(1)}, u32[]{:S(2)}, u32[]{:S(2)}) collective-permute-start(f32[8,1792]{1,0:T(8,128)S(1)} %fusion), channel_id=1, source_target_pairs={{0,56},{4,60},{8,64},{12,68},{16,72},{20,76},{24,80},{28,84},{32,8... | collective-permute-start | bytes 172040
  558.2 23.9 %collective-permute-start.12 = (f32[8,1792]{1,0:T(8,128)S(1)}, f32[8,1792]{1,0:T(8,128)S(1)}, u32[]{:S(2)}, u32[]{:S(2)}) collective-permute-start(f32[8,1792]{1,0:T(8,128)S(1)} %fusion), channel_id=1, source_target_pairs={{0,52},{4,56},{8,60},{12,64},{16,68},{20,72},{24,76},{28,80},{32,8... | collective-permute-start | bytes 172040
  559.5 24.0 %collective-permute-start.11 = (f32[8,1792]{1,0:T(8,128)S(1)}, f32[8,1792]{1,0:T(8,128)S(1)}, u32[]{:S(2)}, u32[]{:S(2)}) collective-permute-start(f32[8,1792]{1,0:T(8,128)S(1)} %fusion), channel_id=1, source_target_pairs={{0,48},{4,52},{8,56},{12,60},{16,64},{20,68},{24,72},{28,76},{32,8... | collective-permute-start | bytes 172040
  560.8 26.4 %collective-permute-start.10 = (f32[8,1792]{1,0:T(8,128)S(1)}, f32[8,1792]{1,0:T(8,128)S(1)}, u32[]{:S(2)}, u32[]{:S(2)}) collective-permute-start(f32[8,1792]{1,0:T(8,128)S(1)} %fusion), channel_id=1, source_target_pairs={{0,44},{4,48},{8,52},{12,56},{16,60},{20,64},{24,68},{28,72},{32,7... | collective-permute-start | bytes 172040
  562.1 28.3 %collective-permute-start.9 = (f32[8,1792]{1,0:T(8,128)S(1)}, f32[8,1792]{1,0:T(8,128)S(1)}, u32[]{:S(2)}, u32[]{:S(2)}) collective-permute-start(f32[8,1792]{1,0:T(8,128)S(1)} %fusion), channel_id=1, source_target_pairs={{0,40},{4,44},{8,48},{12,52},{16,56},{20,60},{24,64},{28,68},{32,7... | collective-permute-start | bytes 172040
  580.8 11.7 %collective-permute-start.8 = (f32[8,1792]{1,0:T(8,128)S(1)}, f32[8,1792]{1,0:T(8,128)S(1)}, u32[]{:S(2)}, u32[]{:S(2)}) collective-permute-start(f32[8,1792]{1,0:T(8,128)S(1)} %fusion), channel_id=1, source_target_pairs={{0,36},{4,40},{8,44},{12,48},{16,52},{20,56},{24,60},{28,64},{32,6... | collective-permute-start | bytes 172040
  582.1 12.6 %collective-permute-start.7 = (f32[8,1792]{1,0:T(8,128)S(1)}, f32[8,1792]{1,0:T(8,128)S(1)}, u32[]{:S(2)}, u32[]{:S(2)}) collective-permute-start(f32[8,1792]{1,0:T(8,128)S(1)} %fusion), channel_id=1, source_target_pairs={{0,32},{4,36},{8,40},{12,44},{16,48},{20,52},{24,56},{28,60},{32,6... | collective-permute-start | bytes 172040
  583.4 20.1 %collective-permute-start.6 = (f32[8,1792]{1,0:T(8,128)S(1)}, f32[8,1792]{1,0:T(8,128)S(1)}, u32[]{:S(2)}, u32[]{:S(2)}) collective-permute-start(f32[8,1792]{1,0:T(8,128)S(1)} %fusion), channel_id=1, source_target_pairs={{0,28},{4,32},{8,36},{12,40},{16,44},{20,48},{24,52},{28,56},{32,6... | collective-permute-start | bytes 172040
  587.2 18.6 %collective-permute-start.5 = (f32[8,1792]{1,0:T(8,128)S(1)}, f32[8,1792]{1,0:T(8,128)S(1)}, u32[]{:S(2)}, u32[]{:S(2)}) collective-permute-start(f32[8,1792]{1,0:T(8,128)S(1)} %fusion), channel_id=1, source_target_pairs={{0,24},{4,28},{8,32},{12,36},{16,40},{20,44},{24,48},{28,52},{32,5... | collective-permute-start | bytes 172040
  590.4 20.1 %collective-permute-start.4 = (f32[8,1792]{1,0:T(8,128)S(1)}, f32[8,1792]{1,0:T(8,128)S(1)}, u32[]{:S(2)}, u32[]{:S(2)}) collective-permute-start(f32[8,1792]{1,0:T(8,128)S(1)} %fusion), channel_id=1, source_target_pairs={{0,20},{4,24},{8,28},{12,32},{16,36},{20,40},{24,44},{28,48},{32,5... | collective-permute-start | bytes 172040
  592.6 18.0 %collective-permute-start.3 = (f32[8,1792]{1,0:T(8,128)S(1)}, f32[8,1792]{1,0:T(8,128)S(1)}, u32[]{:S(2)}, u32[]{:S(2)}) collective-permute-start(f32[8,1792]{1,0:T(8,128)S(1)} %fusion), channel_id=1, source_target_pairs={{0,16},{4,20},{8,24},{12,28},{16,32},{20,36},{24,40},{28,44},{32,4... | collective-permute-start | bytes 172040
  594.7 15.8 %collective-permute-start.2 = (f32[8,1792]{1,0:T(8,128)S(1)}, f32[8,1792]{1,0:T(8,128)S(1)}, u32[]{:S(2)}, u32[]{:S(2)}) collective-permute-start(f32[8,1792]{1,0:T(8,128)S(1)} %fusion), channel_id=1, source_target_pairs={{0,12},{4,16},{8,20},{12,24},{16,28},{20,32},{24,36},{28,40},{32,4... | collective-permute-start | bytes 172040
  603.6 7.0 %collective-permute-start.1 = (f32[8,1792]{1,0:T(8,128)S(1)}, f32[8,1792]{1,0:T(8,128)S(1)}, u32[]{:S(2)}, u32[]{:S(2)}) collective-permute-start(f32[8,1792]{1,0:T(8,128)S(1)} %fusion), channel_id=1, source_target_pairs={{0,8},{4,12},{8,16},{12,20},{16,24},{20,28},{24,32},{28,36},{32,40... | collective-permute-start | bytes 172040
  605.8 4.8 collective-permute-start
Sparse Core Ops, SparseCore 0:
  16.5 94.5 all-gather.5
  120.7 41.3 all-reduce.4
  166.2 98.2 all-gather.3
  272.9 43.5 all-reduce.6
where the time goes:
time: 630 us; the launch traced here: 620 us
  waiting for transfers between devices  276 us (44%)
  blocking collectives  234 us (37%)
  starting transfers between devices  53.2 us (8%)
  local copies, waits for them, and re-layouts  17.2 us (3%)
  matrix products  16.5 us (3%)
  between operations  14.2 us (2%)
  other arithmetic  8.23 us (1%)
    unnamed x1, blocking collectives  234 us
    all_gather x1, waiting for transfers between devices, on_device(): full_state = lax.all_gather(hidden_block, 'dp', axis=1, tiled=True)  99.2 us
    all_gather x1, waiting for transfers between devices, on_device(): lax.all_gather(values, 'dp', axis=0, tiled=True)  91.7 us
    unnamed x16, starting transfers between devices  53 us
    psum x1, waiting for transfers between devices, on_device(): summed = lax.psum(stacked.astype(jnp.bfloat16), 'tp').astype(jnp.float32)  43.8 us
    psum x1, waiting for transfers between devices, on_device(): attention = lax.psum(partial_value, 'tp')  41.5 us
  transfers between devices with their start and end apart: 20, of which 4 were waited for; matrix products, arithmetic and copies ran while one was open for 1% of the time, Pallas kernels for 0%

commit v1 on v0

v1 whole, which is shorter than its diff:
```python
import jax
import jax.numpy as jnp
from jax import lax
from jax.experimental import pallas as pl
from jax.experimental.pallas import tpu as pltpu
from jax.sharding import PartitionSpec as P

MESH = pl.DeviceIdType.MESH
F32 = jnp.float32
BF16 = jnp.bfloat16
SCALE = 192.0 ** (-0.5)
SEMS = 160


def iota(shape, axis):
    return lax.broadcasted_iota(jnp.int32, shape, axis)


def by(value, n):
    return ((value.astype(F32) + 0.5) * (1.0 / n)).astype(jnp.int32)


def dot(a, b):
    return jnp.dot(a, b, preferred_element_type=F32)


def one_hot(hit):
    return jnp.where(hit, 1.0, 0.0).astype(BF16)


def kernel(
    q_hbm, cache_hbm, len_ref, slot_ref, wuv_hbm, wo_hbm, resid_hbm, gain_ref, wg_hbm, wu_hbm, wd_hbm,
    out_ref,
    q_v, cache_v, wuv_v, wo_v, resid_v, wg_v, wu_v, wd_v,
    lat_s, msg_s, abuf, perm_s, z_s, wo_s, r_s, p_s, b_rx,
    cbuf, hid_s, x_s, w_s, ss_s, ss_rx, gu_s, d_rx, act_s,
    pta_s, ptb_s, t_s, hm_s, hm_rx, hid_out,
    e1_s, e1_rx, e2_s, e2_rx, u_s, e3_s, e3_rx,
    sems,
):
    dp, t = lax.axis_index("dp"), lax.axis_index("tp")
    c = lax.rem(dp, 2)
    zh = lax.rem(dp // 2, 2)
    y = lax.rem(dp // 4, 4)
    x = dp // 16
    place = dp // 2
    sib = 1 - c
    other = 1 - zh

    def dev(x_, y_, zh_, c_, t_):
        return (((x_ * 4 + y_) * 2 + zh_) * 2 + c_, t_)

    def turn(v, k):
        return lax.rem(v + k + 4, 4)

    used = [0]

    def sem():
        used[0] += 1
        return sems.at[used[0] - 1]

    sends = []

    def remote(src, dst, ss, rs, to):
        return pltpu.make_async_remote_copy(
            src_ref=src, dst_ref=dst, send_sem=ss, recv_sem=rs, device_id=to, device_id_type=MESH
        )

    def send(src, dst, to, landing):
        ss, rs = sem(), sem()
        cp = remote(src, dst, ss, rs, to)
        cp.start()
        sends.append(cp)
        return remote(src, landing, ss, rs, to)

    def load(src, dst):
        cp = pltpu.make_async_copy(src, dst, sem())
        cp.start()
        return cp

    sib_dev = dev(x, y, zh, sib, t)
    zh_dev = dev(x, y, other, c, t)
    x_dev = [dev(turn(x, k), y, zh, c, t) for k in range(4)]
    y_dev = [dev(x, turn(y, k), zh, c, t) for k in range(4)]
    t_dev = [(dp, turn(t, k)) for k in range(4)]

    q_in = load(q_hbm, q_v)
    cache_in = [load(cache_hbm.at[r], cache_v.at[r]) for r in range(6)]
    wuv_in = [load(wuv_hbm.at[pl.ds(16 * i, 16)], wuv_v.at[pl.ds(16 * i, 16)]) for i in range(2)]
    later = [
        load(resid_hbm, resid_v.at[c]),
        load(wo_hbm, wo_v.at[c]),
        load(wg_hbm, wg_v.at[c]),
        load(wu_hbm, wu_v.at[c]),
        load(wd_hbm.at[pl.ds(0, 256)], wd_v.at[pl.ds(pl.multiple_of(256 * c, 256), 256)]),
        load(wd_hbm.at[pl.ds(256, 32)], wd_v.at[pl.ds(pl.multiple_of(512 + 32 * c, 32), 32)]),
    ]
    barrier = pltpu.get_barrier_semaphore()
    for d in [sib_dev, zh_dev] + x_dev[1:] + y_dev[1:] + t_dev[1:]:
        pl.semaphore_signal(barrier, inc=1, device_id=d, device_id_type=MESH)
    for k in range(4):

        @pl.when(jnp.logical_or(x != t, k != t))
        def _():
            pl.semaphore_signal(barrier, inc=1, device_id=dev(t, y, zh, c, k), device_id_type=MESH)

    for j in range(4):
        lat_s[j, pl.ds(6, 32, 8), :] = jnp.zeros((32, 128), F32)
        lat_s[j, pl.ds(7, 32, 8), :] = jnp.zeros((32, 128), F32)
    q_in.wait()
    for r in range(6):
        cache_in[r].wait()
        keys = cache_v[r]
        scores = (
            lax.dot_general(q_v[r], keys, (((1,), (1,)), ((), ())), preferred_element_type=F32) * SCALE
        )
        live = iota((32, 320), 1) < len_ref[r]
        top = jnp.max(jnp.where(live, scores, -1e30), axis=1, keepdims=True)
        weights = jnp.where(live, jnp.exp(scores - top), 0.0)
        probs = (weights / jnp.sum(weights, axis=1, keepdims=True)).astype(BF16)
        latent = dot(probs, keys[:, :512])
        for j in range(4):
            lat_s[j, pl.ds(r, 32, 8), :] = latent[:, 128 * j : 128 * j + 128]
    for half in range(2):
        wuv_in[half].wait()
        for low in range(8):
            for high in range(2):
                h = half * 16 + low * 2 + high
                latent = [lat_s[j, 8 * h : 8 * h + 8, :].astype(BF16) for j in range(4)]
                value = dot(jnp.concatenate(latent, axis=1), wuv_v[h])
                msg_s[half, 6 * low : 6 * low + 8, 128 * high : 128 * high + 128] = value
        abuf[half, x, y, zh] = msg_s[half, 0:48, :].astype(BF16)

    pl.semaphore_wait(barrier, 15 - jnp.where(x == t, 1, 0))

    def across(buf):
        return send(buf.at[:, x, y, zh], buf.at[:, x, y, zh], zh_dev, buf.at[:, x, y, other])

    def first(buf):
        out = []
        for k in range(1, 4):
            out.append(send(buf.at[0, x, y], buf.at[0, x, y], x_dev[k], buf.at[0, turn(x, -k), y]))
            out.append(send(buf.at[1, x, y], buf.at[1, x, y], y_dev[k], buf.at[1, x, turn(y, -k)]))
        return out

    def second(buf):
        out = []
        for k in range(1, 4):
            out.append(send(buf.at[0, :, y], buf.at[0, :, y], y_dev[k], buf.at[0, :, turn(y, -k)]))
            out.append(send(buf.at[1, x], buf.at[1, x], x_dev[k], buf.at[1, turn(x, -k)]))
        return out

    def arrive(copies):
        for cp in copies:
            cp.wait_recv()

    step = across(abuf)
    for cp in later:
        cp.wait()
    theirs = [
        send(resid_v.at[c], resid_v.at[c], sib_dev, resid_v.at[sib]),
        send(wo_v.at[c], wo_v.at[c], sib_dev, wo_v.at[sib]),
        send(wg_v.at[c], wg_v.at[c], sib_dev, wg_v.at[sib]),
        send(wu_v.at[c], wu_v.at[c], sib_dev, wu_v.at[sib]),
    ]
    for at, n in ((0, 256), (512, 32)):
        mine = wd_v.at[pl.ds(pl.multiple_of(at + n * c, n), n)]
        yours = wd_v.at[pl.ds(pl.multiple_of(at + n * sib, n), n)]
        theirs.append(send(mine, mine, sib_dev, yours))

    row, col = iota((384, 384), 0), iota((384, 384), 1)
    low = by(row, 48)
    within = row - 48 * low
    source = by(within, 6)
    perm_s[...] = one_hot(col == source * 48 + low * 6 + (within - 6 * source))
    slots = jnp.broadcast_to(slot_ref[...], (384, 384))
    half_of = jnp.where(col >= 192, 1, 0)
    rho = col - 192 * half_of
    slot_of = 2 * rho - (rho - 6 * by(rho, 6)) + 6 * half_of
    order = one_hot(row == slot_of)
    rho = iota((384, 192), 1)
    order_c = one_hot(iota((384, 192), 0) == 2 * rho - (rho - 6 * by(rho, 6)) + 6 * c)
    line = iota((256, 384), 0)
    inner = line % 8
    for ref, chip in (
        (pta_s, line // 8),
        (ptb_s, ((line // 16) % 4 * 4 + line // 64) * 2 + (line // 8) % 2),
    ):
        want = jnp.where(inner < 6, (chip * 2 + c) * 6 + inner, -1)
        ref[...] = dot(one_hot(slots[:256] == want), order).astype(BF16)
    line = iota((16, 384), 0)
    want = jnp.where(line % 8 < 6, (place * 2 + line // 8) * 6 + line % 8, -1)
    t_s[...] = dot(one_hot(slots[:16] == want), order_c).astype(BF16)
    moved = dot(one_hot(slots == row), order_c).astype(BF16)

    step.wait_recv()
    step = first(abuf)
    for cp in theirs:
        cp.wait_recv()
    r_s[...] = jnp.zeros((192, 256), F32)
    for k in range(2):
        r_s[:, 128 * k : 128 * k + 112] = lax.dot_general(
            moved, resid_v[k], (((0,), (0,)), ((), ())), preferred_element_type=F32
        )
    wo_s[...] = jnp.zeros((4096, 256), BF16)
    for k in range(2):
        wo_s[:, 128 * k : 128 * k + 112] = wo_v[k]
    arrive(step)
    step = second(abuf)
    w_s[...] = jnp.zeros((2048, 1152), BF16)

    def spread(j, _):
        src = pl.ds(pl.multiple_of(j * 112, 16), 112)
        dst = pl.ds(pl.multiple_of(j * 128, 128), 112)
        w_s[dst, 0:256] = wg_v[0, src, 0:256]
        w_s[dst, 256:512] = wg_v[1, src, 0:256]
        w_s[dst, 512:768] = wu_v[0, src, 0:256]
        w_s[dst, 768:1024] = wu_v[1, src, 0:256]
        for k, (ref, which) in enumerate(((wg_v, 0), (wg_v, 1), (wu_v, 0), (wu_v, 1))):
            w_s[dst, 1024 + 32 * k : 1056 + 32 * k] = ref[which, src, 256:288]
        return 0

    lax.fori_loop(0, 16, spread, 0)
    wd_v[576:640, :] = jnp.zeros((64, 1792), BF16)
    arrive(step)

    for half in range(2):
        for k in range(4):
            packed = abuf[half, k].reshape(384, 256)
            placed = dot(perm_s[...], packed).astype(BF16)
            for low in range(8):
                at = half * 2048 + low * 256
                z_s[48 * k : 48 * k + 48, at : at + 256] = placed[48 * low : 48 * low + 48]
    partial = dot(z_s[...], wo_s[...]) + jnp.where(t == 0, r_s[...], 0.0)
    p_s[...] = partial.astype(BF16).reshape(4, 48, 256)
    b_send, b_recv = [sem() for _ in range(4)], used[0]
    used[0] += 4
    for k in range(4):
        own = jnp.logical_and(x == t, k == x)
        cp = remote(p_s.at[k], b_rx.at[t], b_send[k], sems.at[b_recv + t], dev(k, y, zh, c, x))

        @pl.when(jnp.logical_not(own))
        def _():
            cp.start()

        @pl.when(own)
        def _():
            pltpu.make_async_copy(p_s.at[k], b_rx.at[t], sems.at[b_recv + t]).start()

    for k in range(4):
        pltpu.make_async_copy(p_s.at[k], b_rx.at[k], sems.at[b_recv + k]).wait()
    hidden = jnp.sum(b_rx[...].astype(F32), axis=0).astype(BF16)
    for half in range(2):
        cbuf[half, x, y, zh] = hidden[:, 128 * half : 128 * half + 128]

    across(cbuf).wait_recv()
    arrive(first(cbuf))
    arrive(second(cbuf))
    gain = gain_ref[pl.ds(pl.multiple_of(16 * t, 16), 16), :].astype(F32)
    for k in range(4):
        squares = jnp.zeros((48, 128), F32)
        for j in range(16):
            block = cbuf[j % 2, k, j // 4, (j // 2) % 2]
            hid_s[48 * k : 48 * k + 48, 128 * j : 128 * j + 128] = block
            block = block.astype(F32)
            squares += block * block
            x_s[48 * k : 48 * k + 48, 128 * j : 128 * j + 128] = (block * gain[j : j + 1]).astype(BF16)
        ss_s[k] = jnp.broadcast_to(jnp.sum(squares, axis=1, keepdims=True), (48, 128))
    step = [
        send(ss_s.at[turn(t, k)], ss_rx.at[k - 1], t_dev[k], ss_rx.at[k - 1]) for k in range(1, 4)
    ]

    gu_s[...] = dot(x_s[...], w_s[...]).astype(BF16).reshape(4, 48, 1152)
    step += [
        send(gu_s.at[turn(t, k)], d_rx.at[k - 1], t_dev[k], d_rx.at[k - 1]) for k in range(1, 4)
    ]
    mine = dot(t_s[...], hid_s[...])
    hm_s[...] = mine.reshape(2, 8, 2048)
    hm_in = send(hm_s.at[sib], hm_rx, sib_dev, hm_rx)
    arrive(step)
    total = gu_s[t].astype(F32)
    squares = ss_s[t]
    for k in range(3):
        total += d_rx[k].astype(F32)
        squares += ss_rx[k]
    total *= lax.rsqrt(squares[:, 0:1] * (1.0 / 7168) + 1e-06)

    def silu(v):
        return v * jax.nn.sigmoid(v)

    rest = total[:, 1024:1152]
    tail = silu(rest) * pltpu.roll(rest, 64, 1)
    act_s[c, t, :, 0:512] = (silu(total[:, 0:512]) * total[:, 512:1024]).astype(BF16)
    act_s[c, t, :, 512:640] = jnp.where(iota((48, 128), 1) < 64, tail, 0.0).astype(BF16)
    step = [
        send(act_s.at[c, t], act_s.at[c, t], t_dev[k], act_s.at[c, turn(t, -k)]) for k in range(1, 4)
    ]
    pairs = [send(act_s.at[c, t], act_s.at[c, t], sib_dev, act_s.at[sib, t])]
    hm_in.wait_recv()
    state = hm_s[c] + hm_rx[...]
    for j in range(16):
        hid_out[:, 112 * j : 112 * j + 112] = state[:, 128 * j : 128 * j + 112]
    for k in range(1, 4):
        step[k - 1].wait_recv()
        at = turn(t, -k)
        pairs.append(send(act_s.at[c, at], act_s.at[c, at], sib_dev, act_s.at[sib, at]))
    arrive(pairs)

    everyone = act_s[...].reshape(384, 640)
    for half, ref in ((0, pta_s), (1, ptb_s)):
        rows = dot(ref[...], everyone).astype(BF16)
        down = dot(rows, wd_v[:, 896 * half : 896 * half + 896])
        e1_s[half] = down.astype(BF16).reshape(4, 64, 896)
    spots = (x, y)
    rings = (x_dev, y_dev)
    step = []
    for half in range(2):
        for k in range(1, 4):
            step.append(
                send(
                    e1_s.at[half, turn(spots[half], k)], e1_rx.at[half, k - 1], rings[half][k],
                    e1_rx.at[half, k - 1],
                )
            )
    arrive(step)
    for half in range(2):
        total = e1_s[half, spots[half]].astype(F32)
        for k in range(3):
            total += e1_rx[half, k].astype(F32)
        e2_s[half] = total.astype(BF16).reshape(4, 16, 896)
    step = []
    for half in range(2):
        for k in range(1, 4):
            step.append(
                send(
                    e2_s.at[half, turn(spots[1 - half], k)], e2_rx.at[half, k - 1], rings[1 - half][k],
                    e2_rx.at[half, k - 1],
                )
            )
    arrive(step)
    for half in range(2):
        total = e2_s[half, spots[1 - half]].astype(F32)
        for k in range(3):
            total += e2_rx[half, k].astype(F32)
        u_s[half] = total.reshape(2, 8, 896)
    e3_s[...] = jnp.concatenate([u_s[0, other], u_s[1, other]], axis=0).astype(BF16)
    send(e3_s, e3_rx, zh_dev, e3_rx).wait_recv()
    last = e3_rx[...].astype(F32)
    for half in range(2):
        at = 896 * half
        total = u_s[half, zh] + last[8 * half : 8 * half + 8] + hid_out[:, at : at + 896]
        out_ref[:, at : at + 896] = total[0:6].astype(BF16)

    for k in range(4):

        @pl.when(jnp.logical_not(jnp.logical_and(x == t, k == x)))
        def _():
            remote(p_s.at[k], b_rx.at[t], b_send[k], sems.at[b_recv + t], dev(k, y, zh, c, x)).wait_send()

    for cp in sends:
        cp.wait_send()


def on_device(
    queries, latent_cache, lengths, slot_row, w_uv, w_o, resid, norm_gain, w_gate, w_up, w_down
):
    slots = slot_row.reshape(1, 384)
    gain = jnp.pad(norm_gain.reshape(64, 112), ((0, 0), (0, 16)))
    hbm = pl.BlockSpec(memory_space=pl.ANY)
    vmem = pl.BlockSpec(memory_space=pltpu.VMEM)
    smem = pl.BlockSpec(memory_space=pltpu.SMEM)
    scratch = [
        ((6, 32, 576), BF16),
        ((6, 320, 576), BF16),
        ((32, 512, 128), BF16),
        ((2, 4096, 112), BF16),
        ((2, 384, 112), BF16),
        ((2, 1792, 288), BF16),
        ((2, 1792, 288), BF16),
        ((640, 1792), BF16),
        ((4, 256, 128), F32),
        ((2, 56, 256), F32),
        ((2, 4, 4, 2, 48, 256), BF16),
        ((384, 384), BF16),
        ((192, 4096), BF16),
        ((4096, 256), BF16),
        ((192, 256), F32),
        ((4, 48, 256), BF16),
        ((4, 48, 256), BF16),
        ((2, 4, 4, 2, 48, 128), BF16),
        ((192, 2048), BF16),
        ((192, 2048), BF16),
        ((2048, 1152), BF16),
        ((4, 48, 128), F32),
        ((3, 48, 128), F32),
        ((4, 48, 1152), BF16),
        ((3, 48, 1152), BF16),
        ((2, 4, 48, 640), BF16),
        ((256, 384), BF16),
        ((256, 384), BF16),
        ((16, 192), BF16),
        ((2, 8, 2048), F32),
        ((8, 2048), F32),
        ((8, 1792), F32),
        ((2, 4, 64, 896), BF16),
        ((2, 3, 64, 896), BF16),
        ((2, 4, 16, 896), BF16),
        ((2, 3, 16, 896), BF16),
        ((2, 2, 8, 896), F32),
        ((16, 896), BF16),
        ((16, 896), BF16),
    ]
    return pl.pallas_call(
        kernel,
        out_shape=jax.ShapeDtypeStruct((6, 1792), BF16),
        in_specs=[hbm, hbm, smem, vmem, hbm, hbm, hbm, vmem, hbm, hbm, hbm],
        out_specs=vmem,
        scratch_shapes=[pltpu.VMEM(s, d) for s, d in scratch] + [pltpu.SemaphoreType.DMA((SEMS,))],
        compiler_params=pltpu.CompilerParams(
            collective_id=0, has_side_effects=True, vmem_limit_bytes=58 * 1024 * 1024
        ),
        name="layer",
    )(queries, latent_cache, lengths, slots, w_uv, w_o, resid, gain, w_gate, w_up, w_down)


def solution(mesh):
    placed = (
        P("dp", "tp", None),
        P("dp", None, None),
        P("dp"),
        P(),
        P("tp", None, None),
        P("tp", "dp"),
        P(None, "dp"),
        P(),
        P("tp", "dp"),
        P("tp", "dp"),
        P("dp", "tp"),
    )
    return jax.shard_map(
        on_device, mesh=mesh, in_specs=placed, out_specs=P("dp", "tp"), check_vma=False
    )
```

time: 630 us -> 106 us (0.17); the launches traced: 620 us -> 105 us
  waiting for transfers between devices: 276 us -> 0 us
  blocking collectives: 234 us -> 0 us
  Pallas kernels: 0 us -> 93.6 us
  starting transfers between devices: 53.2 us -> 0 us
  matrix products: 16.5 us -> 0 us
  between operations: 14.2 us -> 0.02 us
  other arithmetic: 8.23 us -> 0 us
    unnamed x1 -> x0, blocking collectives: 234 us -> none
    all_gather x2 -> x0, waiting for transfers between devices: 191 us -> none  [the longest x1 99.2 us: on_device(): full_state = lax.all_gather(hidden_block, 'dp', axis=1, tiled=True)]
    pallas_call x0 -> x1, Pallas kernels: none -> 93.6 us  [on_device(): pl.pallas_call(kernel, out_shape=jax.ShapeDtypeStruct((6, 1792), BF16), i...]
    psum x2 -> x0, waiting for transfers between devices: 85.2 us -> none  [the longest x1 43.8 us: on_device(): summed = lax.psum(stacked.astype(jnp.bfloat16), 'tp').astype(jnp.float32)]
    unnamed x16 -> x0, starting transfers between devices: 53 us -> none
    dot_general x7 -> x0, matrix products: 16.5 us -> none  [the longest x1 3.67 us: on_device(): jnp.dot(lax.all_gather(values, 'dp', axis=0, tiled=True), w_o, preferred_...]
  transfers between devices with their start and end apart: 20 -> 0, of which waited for: 4 -> 0; matrix products, arithmetic and copies ran while one was open for 1% -> 0% of each run, Pallas kernels for 0% -> 0%
where the time goes in v1:
time: 106 us; the launch traced here: 105 us
  Pallas kernels  93.6 us (88%)
  local copies, waits for them, and re-layouts  11.1 us (10%)
    pallas_call x1, Pallas kernels, on_device(): pl.pallas_call(kernel, out_shape=jax.ShapeDtypeStruct((6, 1792), BF16), i...  93.6 us
    unnamed x9, local copies, waits for them, and re-layouts  8.25 us

profile of v1, /device:TPU:32, one launch (start us, length us, event | category | flops | bytes accessed | tf_op | source)
XLA Modules:
  0.0 104.7 jit_solution(6414144007540822033)
XLA Ops:
  0.0 0.0 copy-start.1
  0.0 0.0 copy-start
  0.0 1.4 %reshape.6.slot_ref = s32[1,384]{1,0:T(1,128)} reshape(s32[384]{0:T(512)} %param.14) | data formatting | bytes 3072 | tf_op jit(solution)/shard_map/reshape | solution.py:367
  1.4 0.8 reshape.7
  2.2 0.6 pad.4.gain_ref
  2.8 1.6 %copy.13.resid_hbm = bf16[384,112]{1,0:T(8,128)(2,1)} copy(bf16[384,112]{0,1:T(8,128)(2,1)} %param.17) | data formatting | bytes 172032 | tf_op args[6]
  4.5 2.2 %copy.12.wo_hbm = bf16[4096,112]{1,0:T(8,128)(2,1)} copy(bf16[4096,112]{0,1:T(8,128)(2,1)} %param.16) | data formatting | bytes 1835008 | tf_op args[5]
  6.7 0.0 copy-done
  6.7 1.5 %copy.14.wg_hbm = bf16[1792,288]{1,0:T(8,128)(2,1)} copy(bf16[1792,288]{0,1:T(8,128)(2,1)S(1)} %copy-done) | data formatting | bytes 2064384 | tf_op args[8]
  8.2 0.0 copy-done.1
  8.2 1.5 %copy.15.wu_hbm = bf16[1792,288]{1,0:T(8,128)(2,1)} copy(bf16[1792,288]{0,1:T(8,128)(2,1)S(1)} %copy-done.1) | data formatting | bytes 2064384 | tf_op args[9]
  9.7 93.6 %layer.1 = bf16[6,1792]{1,0:T(8,128)(2,1)} custom-call(bf16[6,32,576]{2,1,0:T(8,128)(2,1)} %q_hbm.1, bf16[6,320,576]{2,1,0:T(8,128)(2,1)} %cache_hbm.1, s32[6]{0:T(128)} %len_ref.1, s32[1,384]{1,0:T(1,128)} %reshape.6.slot_ref, bf16[32,512,128]{2,1,0:T(8,128)(2,1)} %wuv_hbm.1, bf16[4096,112]{1,0:T(8,128)(2,1)} %copy.12.wo_hbm, ...), custom_call_target="tpu_custom_call" | custom-call | tf_op jit(solution)/shard_map/layer/pallas_call | solution.py:413
  103.3 1.4 %copy.17 = bf16[6,1792]{1,0:T(8,128)(2,1)} copy(bf16[6,1792]{1,0:T(8,128)(2,1)} %layer.1) | data formatting | bytes 43008
Async XLA Ops:
  0.0 8.2 %copy-start.1 = (bf16[1792,288]{0,1:T(8,128)(2,1)S(1)}, bf16[1792,288]{0,1:T(8,128)(2,1)}, u32[]{:S(2)}) copy-start(bf16[1792,288]{0,1:T(8,128)(2,1)} %param.20) | copy-start | bytes 3096580
  0.0 6.7 %copy-start = (bf16[1792,288]{0,1:T(8,128)(2,1)S(1)}, bf16[1792,288]{0,1:T(8,128)(2,1)}, u32[]{:S(2)}) copy-start(bf16[1792,288]{0,1:T(8,128)(2,1)} %param.19) | copy-start | bytes 3096580

commit v2 on v1

v2 whole, which is shorter than its diff:
```python
import jax
import jax.numpy as jnp
from jax import lax
from jax.experimental import pallas as pl
from jax.experimental.pallas import tpu as pltpu
from jax.sharding import PartitionSpec as P

MESH = pl.DeviceIdType.MESH
F32 = jnp.float32
BF16 = jnp.bfloat16
SCALE = 192.0 ** (-0.5)
SEMS = 400


def iota(shape, axis):
    return lax.broadcasted_iota(jnp.int32, shape, axis)


def by(value, n):
    return ((value.astype(F32) + 0.5) * (1.0 / n)).astype(jnp.int32)


def dot(a, b):
    return jnp.dot(a, b, preferred_element_type=F32)


def dot_t(a, b):
    return lax.dot_general(a, b, (((1,), (1,)), ((), ())), preferred_element_type=F32)


def one_hot(hit):
    return jnp.where(hit, 1.0, 0.0).astype(BF16)


def kernel(
    q_hbm, cache_hbm, len_hbm, slot_hbm, wuv_hbm, wo_hbm, resid_hbm, gain_hbm, wg_hbm, wu_hbm, wd_hbm,
    out_ref,
    len_ref, slot_ref, gain_ref, gain_s,
    q_v, cache_v, wuv_v, resid_v, wg_v, wu_v, wd_v,
    lat_s, msg_s, abuf, perm_s, z_s, wo_s, slot_s, pt_s, r_s, p_s, b_rx,
    cbuf, hid_s, x_s, w_s, sq_s, ss_s, ss_rx, gu_s, d_rx, act_s,
    turn_s, pad_s, t_s, hid_out,
    e1_s, e1_rx, sum_s, e2_s, e2_rx, u_s, e3_s, e3_rx,
    sems,
):
    dp, t = lax.axis_index("dp"), lax.axis_index("tp")
    c = lax.rem(dp, 2)
    zh = lax.rem(dp // 2, 2)
    y = lax.rem(dp // 4, 4)
    x = dp // 16
    place = dp // 2
    sib = 1 - c
    other = 1 - zh

    def dev(x_, y_, zh_, c_, t_):
        return (((x_ * 4 + y_) * 2 + zh_) * 2 + c_, t_)

    def turn(v, k):
        return lax.rem(v + k + 4, 4)

    used = [0]

    def sem():
        used[0] += 1
        return sems.at[used[0] - 1]

    sends, tails = [], []

    def finish():
        for tail in tails:
            tail()
        for cp in sends:
            cp.wait_send()

    def remote(src, dst, ss, rs, to):
        return pltpu.make_async_remote_copy(
            src_ref=src, dst_ref=dst, send_sem=ss, recv_sem=rs, device_id=to, device_id_type=MESH
        )

    def send(src, dst, to, landing):
        ss, rs = sem(), sem()
        cp = remote(src, dst, ss, rs, to)
        cp.start()
        sends.append(cp)
        return remote(src, landing, ss, rs, to)

    def load(src, dst):
        cp = pltpu.make_async_copy(src, dst, sem())
        cp.start()
        return cp

    sib_dev = dev(x, y, zh, sib, t)
    zh_dev = dev(x, y, other, c, t)
    x_dev = [dev(turn(x, k), y, zh, c, t) for k in range(4)]
    y_dev = [dev(x, turn(y, k), zh, c, t) for k in range(4)]
    t_dev = [(dp, turn(t, k)) for k in range(4)]

    len_in = load(len_hbm, len_ref)
    q_in = load(q_hbm, q_v)
    cache_in = [load(cache_hbm.at[r], cache_v.at[r]) for r in range(6)]
    wuv_in = [load(wuv_hbm.at[pl.ds(16 * i, 16)], wuv_v.at[pl.ds(16 * i, 16)]) for i in range(2)]
    later = [
        load(slot_hbm, slot_ref),
        load(gain_hbm, gain_ref),
        load(resid_hbm, resid_v.at[c]),
        load(wo_hbm, wo_s.at[pl.ds(pl.multiple_of(128 * c, 128), 112)]),
        load(wg_hbm, wg_v.at[c]),
        load(wu_hbm, wu_v.at[c]),
        load(wd_hbm.at[pl.ds(0, 256)], wd_v.at[pl.ds(pl.multiple_of(256 * c, 256), 256)]),
        load(wd_hbm.at[pl.ds(256, 32)], wd_v.at[pl.ds(pl.multiple_of(512 + 32 * c, 32), 32)]),
    ]
    barrier = pltpu.get_barrier_semaphore()
    for d in [sib_dev, zh_dev] + x_dev[1:] + y_dev[1:] + t_dev[1:]:
        pl.semaphore_signal(barrier, inc=1, device_id=d, device_id_type=MESH)
    for k in range(8):

        @pl.when(jnp.logical_or(x != t, zh * 4 + t != k))
        def _():
            pl.semaphore_signal(
                barrier, inc=1, device_id=dev(t, y, k // 4, c, k % 4), device_id_type=MESH
            )

    for j in range(4):
        lat_s[j, pl.ds(6, 32, 8), :] = jnp.zeros((32, 128), F32)
        lat_s[j, pl.ds(7, 32, 8), :] = jnp.zeros((32, 128), F32)
    len_in.wait()
    q_in.wait()
    for r in range(6):
        cache_in[r].wait()
        keys = cache_v[r]
        scores = dot_t(q_v[r], keys) * SCALE
        live = iota((32, 320), 1) < len_ref[r]
        top = jnp.max(jnp.where(live, scores, -1e30), axis=1, keepdims=True)
        weights = jnp.where(live, jnp.exp(scores - top), 0.0)
        probs = (weights / jnp.sum(weights, axis=1, keepdims=True)).astype(BF16)
        latent = dot(probs, keys[:, :512])
        for j in range(4):
            lat_s[j, pl.ds(r, 32, 8), :] = latent[:, 128 * j : 128 * j + 128]
    for half in range(2):
        wuv_in[half].wait()
        for low in range(8):
            for high in range(2):
                h = half * 16 + low * 2 + high
                latent = [lat_s[j, 8 * h : 8 * h + 8, :].astype(BF16) for j in range(4)]
                value = dot(jnp.concatenate(latent, axis=1), wuv_v[h])
                msg_s[half, 6 * low : 6 * low + 8, 128 * high : 128 * high + 128] = value
        abuf[half, x, y, zh] = msg_s[half, 0:48, :].astype(BF16)

    pl.semaphore_wait(barrier, 19 - jnp.where(x == t, 1, 0))

    def arrive(copies):
        for cp in copies:
            cp.wait_recv()

    def first(block):
        out = []
        for k in range(1, 4):
            out.append(send(block(0, x, y), block(0, x, y), x_dev[k], block(0, turn(x, -k), y)))
            out.append(send(block(1, x, y), block(1, x, y), y_dev[k], block(1, x, turn(y, -k))))
        return out

    def second(block):
        out = []
        every = slice(None)
        for k in range(1, 4):
            out.append(send(block(0, every, y), block(0, every, y), y_dev[k], block(0, every, turn(y, -k))))
            out.append(send(block(1, x, every), block(1, x, every), x_dev[k], block(1, turn(x, -k), every)))
        return out

    def near(half, x_, y_):
        return abuf.at[half, x_, y_, zh]

    def far(half, x_, y_):
        return abuf.at[half, x_, y_, other]

    near_in = first(near)
    far_in = send(abuf.at[:, x, y, zh], abuf.at[:, x, y, zh], zh_dev, abuf.at[:, x, y, other])
    for cp in later:
        cp.wait()
    theirs = [
        send(resid_v.at[c], resid_v.at[c], sib_dev, resid_v.at[sib]),
        send(wg_v.at[c], wg_v.at[c], sib_dev, wg_v.at[sib]),
        send(wu_v.at[c], wu_v.at[c], sib_dev, wu_v.at[sib]),
    ]
    for ref, at, step_, n in ((wo_s, 0, 128, 112), (wd_v, 0, 256, 256), (wd_v, 512, 32, 32)):
        ours = ref.at[pl.ds(pl.multiple_of(at + step_ * c, step_), n)]
        other_half = ref.at[pl.ds(pl.multiple_of(at + step_ * sib, step_), n)]
        theirs.append(send(ours, ours, sib_dev, other_half))
    arrive(near_in)
    near_in = second(near)

    row, col = iota((384, 384), 0), iota((384, 384), 1)
    low = by(row, 48)
    within = row - 48 * low
    source = by(within, 6)
    perm_s[...] = one_hot(col == source * 48 + low * 6 + (within - 6 * source))
    far_in.wait_recv()
    far_in = first(far)

    half_of = jnp.where(col >= 192, 1, 0)
    rho = col - 192 * half_of
    slot_of = 2 * rho - (rho - 6 * by(rho, 6)) + 6 * half_of
    order = one_hot(row == slot_of)
    line = iota((192, 384), 0)
    want = ((line % 64) // 2 * 2 + c) * 6 + line // 64 * 2 + line % 2
    slots = jnp.broadcast_to(slot_ref[...][None, :], (192, 384))
    pt_s[...] = dot(one_hot(slots == want), order).astype(BF16)
    rows_here = one_hot(iota((192, 384), 1) == want)
    arrive(far_in)
    far_in = second(far)

    arrive(theirs)
    r_s[...] = jnp.zeros((192, 256), F32)
    for k in range(2):
        r_s[:, 128 * k : 128 * k + 112] = dot_t(rows_here, resid_v[k])
        wo_s[128 * k + 112 : 128 * k + 128, :] = jnp.zeros((16, 4096), BF16)
    gain_s[...] = jnp.zeros((64, 128), F32)
    gains = gain_ref[...].astype(F32)[None, :]
    for j in range(64):
        gain_s[j : j + 1, 0:112] = gains[:, 112 * j : 112 * j + 112]
    line, row = iota((64, 64), 0), iota((64, 64), 1)
    turn_s[...] = one_hot(row == line // 4 % 4 * 16 + line // 16 * 4 + line % 4)
    line, row = iota((64, 48), 0), iota((64, 48), 1)
    pad_s[...] = one_hot(
        jnp.logical_and(line % 8 < 6, row == line % 8 // 2 * 16 + line // 8 * 2 + line % 2)
    )
    line, row = iota((8, 48), 0), iota((8, 48), 1)
    t_s[...] = one_hot(jnp.logical_and(line < 6, row == line // 2 * 16 + (y * 2 + zh) * 2 + line % 2))
    wd_v[576:640, :] = jnp.zeros((64, 1792), BF16)
    w_s[...] = jnp.zeros((1152, 2048), BF16)

    def spread(src, dst):
        for j in range(16):
            dst[:, 128 * j : 128 * j + 112] = src[:, 112 * j : 112 * j + 112]

    for k, ref in enumerate((wg_v, wu_v)):
        for half in range(2):
            at = 512 * k + 256 * half

            def piece(i, _):
                rows = pl.ds(pl.multiple_of(32 * i, 32), 32)
                into = pl.ds(pl.multiple_of(at + 32 * i, 32), 32)
                spread(ref.at[half, rows], w_s.at[into])
                return 0

            lax.fori_loop(0, 8, piece, 0)
            at = 1024 + 64 * k + 32 * half
            spread(ref.at[half, 256:288], w_s.at[at : at + 32])
    arrive(near_in)
    arrive(far_in)

    for half in range(2):
        for k in range(4):
            packed = abuf[half, k].reshape(384, 256)
            placed = dot(perm_s[...], packed).astype(BF16)
            for low in range(8):
                at = half * 2048 + low * 256
                z_s[48 * k : 48 * k + 48, at : at + 256] = placed[48 * low : 48 * low + 48]
    slot_s[c] = dot_t(z_s[...], wo_s[...]).astype(BF16)
    send(slot_s.at[c], slot_s.at[c], sib_dev, slot_s.at[sib]).wait_recv()
    partial = dot(pt_s[...], slot_s[...].reshape(384, 256)) + jnp.where(t == 0, r_s[...], 0.0)
    p_s[...] = partial.astype(BF16).reshape(3, 4, 16, 256)

    b_at = used[0]
    used[0] += 48
    for i in range(3):
        for k in range(4):
            for z_ in range(2):
                own = jnp.logical_and(jnp.logical_and(x == t, k == x), zh == z_)
                arrived = sems.at[b_at + 24 + 8 * i + 4 * zh + t]
                cp = remote(
                    p_s.at[i, k], b_rx.at[i, zh, t], sems.at[b_at + 8 * i + 2 * k + z_], arrived,
                    dev(k, y, z_, c, x),
                )

                @pl.when(jnp.logical_not(own))
                def _():
                    cp.start()

                @pl.when(own)
                def _():
                    pltpu.make_async_copy(p_s.at[i, k], b_rx.at[i, zh, t], arrived).start()

                def sent(cp=cp, own=own):
                    @pl.when(jnp.logical_not(own))
                    def _():
                        cp.wait_send()

                tails.append(sent)

    def blocks(i):
        def block(half, x_, y_):
            return cbuf.at[i, half, x_, y_]

        return block

    step = []
    for i in range(3):
        for z_ in range(2):
            for k in range(4):
                pltpu.make_async_copy(
                    p_s.at[i, k], b_rx.at[i, z_, k], sems.at[b_at + 24 + 8 * i + 4 * z_ + k]
                ).wait()
            hidden = jnp.sum(b_rx[i, z_].astype(F32), axis=0).astype(BF16)
            for half in range(2):
                cbuf[i, half, x, y, z_] = hidden[:, 128 * half : 128 * half + 128]
        step.append(first(blocks(i)))
    for i in range(3):
        arrive(step[i])
        step[i] = second(blocks(i))

    gain = gain_s[pl.ds(pl.multiple_of(16 * t, 16), 16), :]

    def silu(v):
        return v * jax.nn.sigmoid(v)

    def gate_up(i):
        arrive(step[i])
        for k in range(4):
            squares = jnp.zeros((16, 128), F32)
            for j in range(16):
                block = cbuf[i, j % 2, k, j // 4, (j // 2) % 2].astype(F32)
                squares += block * block
                x_s[i, 16 * k : 16 * k + 16, 128 * j : 128 * j + 128] = (block * gain[j : j + 1]).astype(BF16)
            sq_s[16 * k : 16 * k + 16] = squares
        ss_s[i] = lax.dot_general(
            jnp.ones((8, 128), F32), sq_s[...], (((1,), (1,)), ((), ())),
            precision=lax.Precision.HIGHEST, preferred_element_type=F32,
        )
        out = [send(ss_s.at[i], ss_rx.at[i, k - 1], t_dev[k], ss_rx.at[i, k - 1]) for k in range(1, 4)]
        gu_s[i] = dot_t(x_s[i], w_s[...]).astype(BF16).reshape(4, 16, 1152)
        for k in range(1, 4):
            out.append(send(gu_s.at[i, turn(t, k)], d_rx.at[i, k - 1], t_dev[k], d_rx.at[i, k - 1]))
        return out

    def activate(i, copies):
        arrive(copies)
        total = gu_s[i, t].astype(F32)
        squares = ss_s[i]
        for k in range(3):
            total += d_rx[i, k].astype(F32)
            squares += ss_rx[i, k]
        here = iota((16, 64), 1) == 16 * t + iota((16, 64), 0)
        squares = jnp.sum(jnp.where(here, squares[0:1], 0.0), axis=1, keepdims=True)
        total *= lax.rsqrt(squares * (1.0 / 7168) + 1e-06)
        rest = total[:, 1024:1152]
        tail = silu(rest) * pltpu.roll(rest, 64, 1)
        act_s[i, t, :, 0:512] = (silu(total[:, 0:512]) * total[:, 512:1024]).astype(BF16)
        act_s[i, t, :, 512:640] = jnp.where(iota((16, 128), 1) < 64, tail, 0.0).astype(BF16)
        return [
            send(act_s.at[i, t], act_s.at[i, t], t_dev[k], act_s.at[i, turn(t, -k)]) for k in range(1, 4)
        ]

    spots = (x, y)
    rings = (x_dev, y_dev)

    def down(i, copies):
        arrive(copies)
        rows = act_s[i].reshape(64, 640)
        out = []
        for half in range(2):
            if half == 1:
                rows = dot(turn_s[...], rows).astype(BF16)
            part = dot(rows, wd_v[:, 896 * half : 896 * half + 896])
            e1_s[i, half] = part.astype(BF16).reshape(4, 16, 896)
            for k in range(1, 4):
                out.append(
                    send(
                        e1_s.at[i, half, turn(spots[half], k)], e1_rx.at[i, half, k - 1], rings[half][k],
                        e1_rx.at[i, half, k - 1],
                    )
                )
        return out

    def collect(i, copies):
        arrive(copies)
        for half in range(2):
            total = e1_s[i, half, spots[half]].astype(F32)
            for k in range(3):
                total += e1_rx[i, half, k].astype(F32)
            sum_s[half, 16 * i : 16 * i + 16] = total.astype(BF16)

    wide = [gate_up(0), gate_up(1)]
    thin = [activate(0, wide[0])]
    wide.append(gate_up(2))
    thin.append(activate(1, wide[1]))
    ends = [down(0, thin[0])]
    thin.append(activate(2, wide[2]))
    for i in range(3):
        for j in range(16):
            hid_s[16 * i : 16 * i + 16, 128 * j : 128 * j + 128] = cbuf[i, j % 2, x, j // 4, (j // 2) % 2]
    state = dot(t_s[...], hid_s[...])
    for j in range(16):
        hid_out[:, 112 * j : 112 * j + 112] = state[:, 128 * j : 128 * j + 112]
    ends.append(down(1, thin[1]))
    collect(0, ends[0])
    ends.append(down(2, thin[2]))
    collect(1, ends[1])
    collect(2, ends[2])
    step = []
    for half in range(2):
        e2_s[half] = dot(pad_s[...], sum_s[half]).astype(BF16).reshape(4, 16, 896)
        for k in range(1, 4):
            step.append(
                send(
                    e2_s.at[half, turn(spots[1 - half], k)], e2_rx.at[half, k - 1], rings[1 - half][k],
                    e2_rx.at[half, k - 1],
                )
            )
    arrive(step)
    for half in range(2):
        total = e2_s[half, spots[1 - half]].astype(F32)
        for k in range(3):
            total += e2_rx[half, k].astype(F32)
        u_s[half] = total.reshape(2, 8, 896)
    e3_s[...] = jnp.concatenate([u_s[0, other], u_s[1, other]], axis=0).astype(BF16)
    send(e3_s, e3_rx, zh_dev, e3_rx).wait_recv()
    last = e3_rx[...].astype(F32)
    for half in range(2):
        at = 896 * half
        total = u_s[half, zh] + last[8 * half : 8 * half + 8] + hid_out[:, at : at + 896]
        out_ref[:, at : at + 896] = total[0:6].astype(BF16)
    finish()


def on_device(
    queries, latent_cache, lengths, slot_row, w_uv, w_o, resid, norm_gain, w_gate, w_up, w_down
):
    hbm = pl.BlockSpec(memory_space=pl.ANY)
    vmem = pl.BlockSpec(memory_space=pltpu.VMEM)
    scratch = [
        ((384,), jnp.int32),
        ((7168,), BF16),
        ((64, 128), F32),
        ((6, 32, 576), BF16),
        ((6, 320, 576), BF16),
        ((32, 512, 128), BF16),
        ((2, 112, 384), BF16),
        ((2, 288, 1792), BF16),
        ((2, 288, 1792), BF16),
        ((640, 1792), BF16),
        ((4, 256, 128), F32),
        ((2, 56, 256), F32),
        ((2, 4, 4, 2, 48, 256), BF16),
        ((384, 384), BF16),
        ((192, 4096), BF16),
        ((256, 4096), BF16),
        ((2, 192, 256), BF16),
        ((192, 384), BF16),
        ((192, 256), F32),
        ((3, 4, 16, 256), BF16),
        ((3, 2, 4, 16, 256), BF16),
        ((3, 2, 4, 4, 2, 16, 128), BF16),
        ((48, 2048), BF16),
        ((3, 64, 2048), BF16),
        ((1152, 2048), BF16),
        ((64, 128), F32),
        ((3, 8, 64), F32),
        ((3, 3, 8, 64), F32),
        ((3, 4, 16, 1152), BF16),
        ((3, 3, 16, 1152), BF16),
        ((3, 4, 16, 640), BF16),
        ((64, 64), BF16),
        ((64, 48), BF16),
        ((8, 48), BF16),
        ((8, 1792), F32),
        ((3, 2, 4, 16, 896), BF16),
        ((3, 2, 3, 16, 896), BF16),
        ((2, 48, 896), BF16),
        ((2, 4, 16, 896), BF16),
        ((2, 3, 16, 896), BF16),
        ((2, 2, 8, 896), F32),
        ((16, 896), BF16),
        ((16, 896), BF16),
    ]
    return pl.pallas_call(
        kernel,
        out_shape=jax.ShapeDtypeStruct((6, 1792), BF16),
        in_specs=[hbm] * 11,
        out_specs=vmem,
        scratch_shapes=[pltpu.SMEM((6,), jnp.int32)]
        + [pltpu.VMEM(s, d) for s, d in scratch]
        + [pltpu.SemaphoreType.DMA((SEMS,))],
        compiler_params=pltpu.CompilerParams(
            collective_id=0, has_side_effects=True, vmem_limit_bytes=58 * 1024 * 1024
        ),
        name="layer",
    )(
        queries, latent_cache, lengths, slot_row, w_uv, w_o.T, resid.T, norm_gain, w_gate.T, w_up.T, w_down
    )


def solution(mesh):
    placed = (
        P("dp", "tp", None),
        P("dp", None, None),
        P("dp"),
        P(),
        P("tp", None, None),
        P("tp", "dp"),
        P(None, "dp"),
        P(),
        P("tp", "dp"),
        P("tp", "dp"),
        P("dp", "tp"),
    )
    return jax.shard_map(
        on_device, mesh=mesh, in_specs=placed, out_specs=P("dp", "tp"), check_vma=False
    )
```

time: 106 us -> 91.4 us (0.86); the launches traced: 105 us -> 91.2 us
  local copies, waits for them, and re-layouts: 11.1 us -> 1.36 us
  Pallas kernels: 93.6 us -> 89.9 us
    unnamed x9 -> x1, local copies, waits for them, and re-layouts: 8.25 us -> 1.36 us
    pallas_call x1, Pallas kernels: 93.6 us -> 89.9 us  [on_device(): pl.pallas_call(kernel, out_shape=jax.ShapeDtypeStruct((6, 1792), BF16), i...]
    reshape x2 -> x0, local copies, waits for them, and re-layouts: 2.22 us -> none  [the longest x1 1.42 us: on_device(): slots = slot_row.reshape(1, 384)]
where the time goes in v2:
time: 91.4 us; the launch traced here: 91.2 us
  Pallas kernels  89.9 us (98%)
  local copies, waits for them, and re-layouts  1.36 us (1%)
    pallas_call x1, Pallas kernels, on_device(): pl.pallas_call(kernel, out_shape=jax.ShapeDtypeStruct((6, 1792), BF16), i...  89.9 us

profile of v2, /device:TPU:32, one launch (start us, length us, event | category | flops | bytes accessed | tf_op | source)
XLA Modules:
  0.0 91.2 jit_solution(4310084188369040616)
XLA Ops:
  0.0 89.9 %layer.1 = bf16[6,1792]{1,0:T(8,128)(2,1)} custom-call(bf16[6,32,576]{2,1,0:T(8,128)(2,1)} %q_hbm.1, bf16[6,320,576]{2,1,0:T(8,128)(2,1)} %cache_hbm.1, s32[6]{0:T(128)} %len_hbm.1, s32[384]{0:T(512)} %slot_hbm.1, bf16[32,512,128]{2,1,0:T(8,128)(2,1)} %wuv_hbm.1, bf16[112,4096]{1,0:T(8,128)(2,1)} %bitcast.6, bf16[112,384]{1,0:T(8,128)(2,1)} %bitcast.7, ...), custom_call_target="tpu_custom_call" | custom-call | tf_op jit(solution)/shard_map/layer/pallas_call | solution.py:476
  89.9 1.4 %copy.13 = bf16[6,1792]{1,0:T(8,128)(2,1)} copy(bf16[6,1792]{1,0:T(8,128)(2,1)} %layer.1) | data formatting | bytes 43008

commit v3 on v2

v3 whole, which is shorter than its diff:
```python
import jax
import jax.numpy as jnp
from jax import lax
from jax.experimental import pallas as pl
from jax.experimental.pallas import tpu as pltpu
from jax.sharding import PartitionSpec as P

MESH = pl.DeviceIdType.MESH
F32 = jnp.float32
BF16 = jnp.bfloat16
SCALE = 192.0 ** (-0.5)
SEMS = 88


def iota(shape, axis):
    return lax.broadcasted_iota(jnp.int32, shape, axis)


def by(value, n):
    return ((value.astype(F32) + 0.5) * (1.0 / n)).astype(jnp.int32)


def dot(a, b):
    return jnp.dot(a, b, preferred_element_type=F32)


def dot_t(a, b):
    return lax.dot_general(a, b, (((1,), (1,)), ((), ())), preferred_element_type=F32)


def one_hot(hit):
    return jnp.where(hit, 1.0, 0.0).astype(BF16)


def kernel(
    q_hbm, cache_hbm, len_hbm, slot_hbm, wuv_hbm, wo_hbm, resid_hbm, gain_hbm, wg_hbm, wu_hbm, wd_hbm,
    out_ref,
    len_ref, slot_ref, gain_ref, gain_s,
    q_v, cache_v, wuv_v, resid_v, w_raw, wd_v,
    lat_s, msg_s, abuf, perm_s, z_s, wo_s, slot_s, pt_s, r_s, p_s, b_rx,
    cbuf, hid_s, x_s, w_s, sq_s, ss_s, ss_rx, gu_s, d_rx, act_s,
    turn_s, pad_s, t_s, hid_out,
    e1_s, e1_rx, sum_s, e2_s, e2_rx, u_s, e3_s, e3_rx,
    sems,
):
    dp, t = lax.axis_index("dp"), lax.axis_index("tp")
    c = lax.rem(dp, 2)
    zh = lax.rem(dp // 2, 2)
    y = lax.rem(dp // 4, 4)
    x = dp // 16
    place = dp // 2
    sib = 1 - c
    other = 1 - zh

    def dev(x_, y_, zh_, c_, t_):
        return (((x_ * 4 + y_) * 2 + zh_) * 2 + c_, t_)

    def turn(v, k):
        return lax.rem(v + k + 4, 4)

    used = [0]

    def sem():
        used[0] += 1
        return sems.at[used[0] - 1]

    sends, tails = [], []

    def finish():
        for tail in tails:
            tail()
        for cp in sends:
            cp.wait()

    def remote(src, dst, ss, rs, to):
        return pltpu.make_async_remote_copy(
            src_ref=src, dst_ref=dst, send_sem=ss, recv_sem=rs, device_id=to, device_id_type=MESH
        )

    def group(copies, whole):
        ss, rs = sem(), sem()
        for src, dst, to in copies:
            remote(src, dst, ss, rs, to).start()
        sends.append(pltpu.make_async_copy(whole, whole, ss))
        return landing(whole, rs)

    def landing(whole, rs):
        return pltpu.make_async_copy(whole, whole, rs)

    def send(src, dst, to, lands):
        return group([(src, dst, to)], lands)

    def load(src, dst):
        cp = pltpu.make_async_copy(src, dst, sem())
        cp.start()
        return cp

    sib_dev = dev(x, y, zh, sib, t)
    zh_dev = dev(x, y, other, c, t)
    x_dev = [dev(turn(x, k), y, zh, c, t) for k in range(4)]
    y_dev = [dev(x, turn(y, k), zh, c, t) for k in range(4)]
    t_dev = [(dp, turn(t, k)) for k in range(4)]

    len_in = load(len_hbm, len_ref)
    q_in = load(q_hbm, q_v)
    cache_in = load(cache_hbm, cache_v)
    wuv_in = [load(wuv_hbm.at[pl.ds(16 * i, 16)], wuv_v.at[pl.ds(16 * i, 16)]) for i in range(2)]
    later = [
        load(slot_hbm, slot_ref),
        load(gain_hbm, gain_ref),
        load(resid_hbm, resid_v.at[c]),
        load(wo_hbm, wo_s.at[pl.ds(pl.multiple_of(128 * c, 128), 112)]),
        load(wg_hbm, w_raw.at[0, c]),
        load(wu_hbm, w_raw.at[1, c]),
        load(wd_hbm.at[pl.ds(0, 256)], wd_v.at[pl.ds(pl.multiple_of(256 * c, 256), 256)]),
        load(wd_hbm.at[pl.ds(256, 32)], wd_v.at[pl.ds(pl.multiple_of(512 + 32 * c, 32), 32)]),
    ]
    barrier = pltpu.get_barrier_semaphore()
    for d in [sib_dev, zh_dev] + x_dev[1:] + y_dev[1:] + t_dev[1:]:
        pl.semaphore_signal(barrier, inc=1, device_id=d, device_id_type=MESH)
    for k in range(8):

        @pl.when(jnp.logical_or(x != t, zh * 4 + t != k))
        def _():
            pl.semaphore_signal(
                barrier, inc=1, device_id=dev(t, y, k // 4, c, k % 4), device_id_type=MESH
            )

    for j in range(4):
        lat_s[j, pl.ds(6, 32, 8), :] = jnp.zeros((32, 128), F32)
        lat_s[j, pl.ds(7, 32, 8), :] = jnp.zeros((32, 128), F32)
    len_in.wait()
    q_in.wait()
    cache_in.wait()
    scores = []
    for r in range(6):
        live = iota((32, 320), 1) < len_ref[r]
        scores.append(jnp.where(live, dot_t(q_v[r], cache_v[r]) * SCALE, -1e30))
    scores = jnp.concatenate(scores, axis=0)
    weights = jnp.exp(scores - jnp.max(scores, axis=1, keepdims=True))
    probs = (weights * (1.0 / jnp.sum(weights, axis=1, keepdims=True))).astype(BF16)
    for r in range(6):
        latent = dot(probs[32 * r : 32 * r + 32], cache_v[r, :, :512])
        for j in range(4):
            lat_s[j, pl.ds(r, 32, 8), :] = latent[:, 128 * j : 128 * j + 128]
    for half in range(2):
        wuv_in[half].wait()
        for low in range(8):
            for high in range(2):
                h = half * 16 + low * 2 + high
                latent = [lat_s[j, 8 * h : 8 * h + 8, :].astype(BF16) for j in range(4)]
                value = dot(jnp.concatenate(latent, axis=1), wuv_v[h])
                msg_s[half, 6 * low : 6 * low + 8, 128 * high : 128 * high + 128] = value
        abuf[half, zh, x, y] = msg_s[half, 0:48, :].astype(BF16)

    pl.semaphore_wait(barrier, 19 - jnp.where(x == t, 1, 0))

    every = slice(None)

    def first(block, whole):
        out = []
        for k in range(1, 4):
            out.append((block(0, x, y), block(0, x, y), x_dev[k]))
            out.append((block(1, x, y), block(1, x, y), y_dev[k]))
        return group(out, whole)

    def second(block, whole):
        out = []
        for k in range(1, 4):
            out.append((block(0, every, y), block(0, every, y), y_dev[k]))
            out.append((block(1, x, every), block(1, x, every), x_dev[k]))
        return group(out, whole)

    def near(half, x_, y_):
        return abuf.at[half, zh, x_, y_]

    def far(half, x_, y_):
        return abuf.at[half, other, x_, y_]

    six, twenty_four = abuf.at[0, 0, 0:3, 0:2], abuf.at[0:2, 0, 0:3]
    near_in = first(near, six)
    far_in = send(abuf.at[:, zh, x, y], abuf.at[:, zh, x, y], zh_dev, abuf.at[:, other, x, y])
    for cp in later:
        cp.wait()
    theirs = [
        send(resid_v.at[c], resid_v.at[c], sib_dev, resid_v.at[sib]),
        send(w_raw.at[:, c], w_raw.at[:, c], sib_dev, w_raw.at[:, sib]),
    ]
    for ref, at, step_, n in ((wo_s, 0, 128, 112), (wd_v, 0, 256, 256), (wd_v, 512, 32, 32)):
        ours = ref.at[pl.ds(pl.multiple_of(at + step_ * c, step_), n)]
        other_half = ref.at[pl.ds(pl.multiple_of(at + step_ * sib, step_), n)]
        theirs.append(send(ours, ours, sib_dev, other_half))
    row, col = iota((384, 384), 0), iota((384, 384), 1)
    low = by(row, 48)
    within = row - 48 * low
    source = by(within, 6)
    perm_s[...] = one_hot(col == source * 48 + low * 6 + (within - 6 * source))
    near_in.wait()
    near_in = second(near, twenty_four)

    half_of = jnp.where(col >= 192, 1, 0)
    rho = col - 192 * half_of
    z_of = jnp.where(rho >= 96, 1, 0)
    rho -= 96 * z_of
    chip = by(rho, 6)
    order = one_hot(row == ((chip * 2 + z_of) * 2 + half_of) * 6 + (rho - 6 * chip))
    line = iota((192, 384), 0)
    want = ((line % 64) // 2 * 2 + c) * 6 + line // 64 * 2 + line % 2
    slots = jnp.broadcast_to(slot_ref[...][None, :], (192, 384))
    pt_s[...] = dot(one_hot(slots == want), order).astype(BF16)
    rows_here = one_hot(iota((192, 384), 1) == want)
    far_in.wait()
    far_in = first(far, six)

    for cp in theirs:
        cp.wait()
    r_s[...] = jnp.zeros((192, 256), F32)
    for k in range(2):
        r_s[:, 128 * k : 128 * k + 112] = dot_t(rows_here, resid_v[k])
        wo_s[128 * k + 112 : 128 * k + 128, :] = jnp.zeros((16, 4096), BF16)
    gain_s[...] = jnp.zeros((64, 128), F32)
    gains = gain_ref[...].astype(F32)[None, :]
    for j in range(64):
        gain_s[j : j + 1, 0:112] = gains[:, 112 * j : 112 * j + 112]
    line, row = iota((64, 64), 0), iota((64, 64), 1)
    turn_s[...] = one_hot(row == line // 4 % 4 * 16 + line // 16 * 4 + line % 4)
    line, row = iota((64, 48), 0), iota((64, 48), 1)
    pad_s[...] = one_hot(
        jnp.logical_and(line % 8 < 6, row == line % 8 // 2 * 16 + line // 8 * 2 + line % 2)
    )
    line, row = iota((8, 48), 0), iota((8, 48), 1)
    t_s[...] = one_hot(jnp.logical_and(line < 6, row == line // 2 * 16 + (y * 2 + zh) * 2 + line % 2))
    wd_v[576:640, :] = jnp.zeros((64, 1792), BF16)
    far_in.wait()
    far_in = second(far, twenty_four)

    def spread(block, part, at):
        width = block.shape[1]
        for j in range(8):
            row = 1024 * part + 128 * j
            w_s[row : row + 112, at : at + width] = block[112 * j : 112 * j + 112]

    for j in range(16):
        w_s[128 * j + 112 : 128 * j + 128, :] = jnp.zeros((16, 1152), BF16)
    for part in range(2):
        cols = slice(896 * part, 896 * part + 896)
        for k in range(2):
            for half in range(2):
                spread(w_raw[k, half, 0:256, cols].T, part, 512 * k + 256 * half)
        rest = [w_raw[k, half, 256:288, cols] for k in range(2) for half in range(2)]
        spread(jnp.concatenate(rest, axis=0).T, part, 1024)

    def project(z_):
        for half in range(2):
            for k in range(2):
                packed = abuf[half, z_, 2 * k : 2 * k + 2].reshape(384, 256)
                placed = dot(perm_s[...], packed).astype(BF16)
                for low in range(8):
                    at = half * 2048 + low * 256
                    z_s[48 * k : 48 * k + 48, at : at + 256] = placed[48 * low : 48 * low + 48]
        slot_s[c, z_] = dot_t(z_s[...], wo_s[...]).astype(BF16)
        return send(slot_s.at[c, z_], slot_s.at[c, z_], sib_dev, slot_s.at[sib, z_])

    near_in.wait()
    step = [project(zh)]
    far_in.wait()
    step.append(project(other))
    for cp in step:
        cp.wait()
    partial = dot(pt_s[...], slot_s[...].reshape(384, 256)) + jnp.where(t == 0, r_s[...], 0.0)
    p_s[...] = partial.astype(BF16).reshape(12, 16, 256)

    b_sent, b_in = sem(), [sem() for _ in range(3)]
    for i in range(3):
        for k in range(4):
            for z_ in range(2):
                own = jnp.logical_and(jnp.logical_and(x == t, k == x), zh == z_)
                src, dst = p_s.at[4 * i + k], b_rx.at[8 * i + 4 * zh + t]

                @pl.when(jnp.logical_not(own))
                def _():
                    remote(src, dst, b_sent, b_in[i], dev(k, y, z_, c, x)).start()

                @pl.when(own)
                def _():
                    pltpu.make_async_copy(src, dst, b_in[i]).start()

    def sent():
        for n, when in ((24, x != t), (21, x == t)):

            @pl.when(when)
            def _():
                pltpu.make_async_copy(b_rx.at[0:n], b_rx.at[0:n], b_sent).wait()

    tails.append(sent)

    def blocks(i):
        def block(half, x_, y_):
            return cbuf.at[i, half, x_, y_]

        return block

    step = []
    for i in range(3):
        landing(b_rx.at[8 * i : 8 * i + 8], b_in[i]).wait()
        for z_ in range(2):
            at = 8 * i + 4 * z_
            hidden = jnp.sum(b_rx[at : at + 4].astype(F32), axis=0).astype(BF16)
            for half in range(2):
                cbuf[i, half, x, y, z_] = hidden[:, 128 * half : 128 * half + 128]
        step.append(first(blocks(i), cbuf.at[i, 0, 0:3, 0:2]))
    for i in range(3):
        step[i].wait()
        step[i] = second(blocks(i), cbuf.at[i, 0:2, 0:3])

    gain = gain_s[pl.ds(pl.multiple_of(16 * t, 16), 16), :]

    def silu(v):
        return v * jax.nn.sigmoid(v)

    def gate_up(i):
        step[i].wait()
        for k in range(4):
            squares = jnp.zeros((16, 128), F32)
            for j in range(16):
                block = cbuf[i, j % 2, k, j // 4, (j // 2) % 2].astype(F32)
                squares += block * block
                x_s[i, 16 * k : 16 * k + 16, 128 * j : 128 * j + 128] = (block * gain[j : j + 1]).astype(BF16)
            sq_s[16 * k : 16 * k + 16] = squares
        ss_s[i] = lax.dot_general(
            jnp.ones((8, 128), F32), sq_s[...], (((1,), (1,)), ((), ())),
            precision=lax.Precision.HIGHEST, preferred_element_type=F32,
        )
        out = [group([(ss_s.at[i], ss_rx.at[i, k - 1], t_dev[k]) for k in range(1, 4)], ss_rx.at[i])]
        gu_s[i] = dot(x_s[i], w_s[...]).astype(BF16).reshape(4, 16, 1152)
        parts = [(gu_s.at[i, turn(t, k)], d_rx.at[i, k - 1], t_dev[k]) for k in range(1, 4)]
        out.append(group(parts, d_rx.at[i]))
        return out

    def activate(i, copies):
        for cp in copies:
            cp.wait()
        total = gu_s[i, t].astype(F32)
        squares = ss_s[i]
        for k in range(3):
            total += d_rx[i, k].astype(F32)
            squares += ss_rx[i, k]
        here = iota((16, 64), 1) == 16 * t + iota((16, 64), 0)
        squares = jnp.sum(jnp.where(here, squares[0:1], 0.0), axis=1, keepdims=True)
        total *= lax.rsqrt(squares * (1.0 / 7168) + 1e-06)
        rest = total[:, 1024:1152]
        tail = silu(rest) * pltpu.roll(rest, 64, 1)
        act_s[i, t, :, 0:512] = (silu(total[:, 0:512]) * total[:, 512:1024]).astype(BF16)
        act_s[i, t, :, 512:640] = jnp.where(iota((16, 128), 1) < 64, tail, 0.0).astype(BF16)
        mine = act_s.at[i, t]
        return group([(mine, mine, t_dev[k]) for k in range(1, 4)], act_s.at[i, 0:3])

    spots = (x, y)
    rings = (x_dev, y_dev)

    def down(i, copies):
        copies.wait()
        rows = act_s[i].reshape(64, 640)
        out = []
        for half in range(2):
            if half == 1:
                rows = dot(turn_s[...], rows).astype(BF16)
            part = dot(rows, wd_v[:, 896 * half : 896 * half + 896])
            e1_s[i, half] = part.astype(BF16).reshape(4, 16, 896)
            for k in range(1, 4):
                out.append((e1_s.at[i, half, turn(spots[half], k)], e1_rx.at[i, half, k - 1], rings[half][k]))
        return group(out, e1_rx.at[i])

    def collect(i, copies):
        copies.wait()
        for half in range(2):
            total = e1_s[i, half, spots[half]].astype(F32)
            for k in range(3):
                total += e1_rx[i, half, k].astype(F32)
            sum_s[half, 16 * i : 16 * i + 16] = total.astype(BF16)

    wide = [gate_up(i) for i in range(3)]
    for i in range(3):
        for j in range(16):
            hid_s[16 * i : 16 * i + 16, 128 * j : 128 * j + 128] = cbuf[i, j % 2, x, j // 4, (j // 2) % 2]
    state = dot(t_s[...], hid_s[...])
    for j in range(16):
        hid_out[:, 112 * j : 112 * j + 112] = state[:, 128 * j : 128 * j + 112]
    thin = [activate(i, wide[i]) for i in range(3)]
    ends = [down(0, thin[0]), down(1, thin[1])]
    collect(0, ends[0])
    ends.append(down(2, thin[2]))
    collect(1, ends[1])
    collect(2, ends[2])
    step = []
    for half in range(2):
        e2_s[half] = dot(pad_s[...], sum_s[half]).astype(BF16).reshape(4, 16, 896)
        for k in range(1, 4):
            to = rings[1 - half][k]
            step.append((e2_s.at[half, turn(spots[1 - half], k)], e2_rx.at[half, k - 1], to))
    group(step, e2_rx).wait()
    for half in range(2):
        total = e2_s[half, spots[1 - half]].astype(F32)
        for k in range(3):
            total += e2_rx[half, k].astype(F32)
        u_s[half] = total.reshape(2, 8, 896)
    e3_s[...] = jnp.concatenate([u_s[0, other], u_s[1, other]], axis=0).astype(BF16)
    send(e3_s, e3_rx, zh_dev, e3_rx).wait()
    last = e3_rx[...].astype(F32)
    for half in range(2):
        at = 896 * half
        total = u_s[half, zh] + last[8 * half : 8 * half + 8] + hid_out[:, at : at + 896]
        out_ref[:, at : at + 896] = total[0:6].astype(BF16)
    finish()


def on_device(
    queries, latent_cache, lengths, slot_row, w_uv, w_o, resid, norm_gain, w_gate, w_up, w_down
):
    hbm = pl.BlockSpec(memory_space=pl.ANY)
    vmem = pl.BlockSpec(memory_space=pltpu.VMEM)
    scratch = [
        ((384,), jnp.int32),
        ((7168,), BF16),
        ((64, 128), F32),
        ((6, 32, 576), BF16),
        ((6, 320, 576), BF16),
        ((32, 512, 128), BF16),
        ((2, 112, 384), BF16),
        ((2, 2, 288, 1792), BF16),
        ((640, 1792), BF16),
        ((4, 256, 128), F32),
        ((2, 56, 256), F32),
        ((2, 2, 4, 4, 48, 256), BF16),
        ((384, 384), BF16),
        ((96, 4096), BF16),
        ((256, 4096), BF16),
        ((2, 2, 96, 256), BF16),
        ((192, 384), BF16),
        ((192, 256), F32),
        ((12, 16, 256), BF16),
        ((24, 16, 256), BF16),
        ((3, 2, 4, 4, 2, 16, 128), BF16),
        ((48, 2048), BF16),
        ((3, 64, 2048), BF16),
        ((2048, 1152), BF16),
        ((64, 128), F32),
        ((3, 8, 64), F32),
        ((3, 3, 8, 64), F32),
        ((3, 4, 16, 1152), BF16),
        ((3, 3, 16, 1152), BF16),
        ((3, 4, 16, 640), BF16),
        ((64, 64), BF16),
        ((64, 48), BF16),
        ((8, 48), BF16),
        ((8, 1792), F32),
        ((3, 2, 4, 16, 896), BF16),
        ((3, 2, 3, 16, 896), BF16),
        ((2, 48, 896), BF16),
        ((2, 4, 16, 896), BF16),
        ((2, 3, 16, 896), BF16),
        ((2, 2, 8, 896), F32),
        ((16, 896), BF16),
        ((16, 896), BF16),
    ]
    return pl.pallas_call(
        kernel,
        out_shape=jax.ShapeDtypeStruct((6, 1792), BF16),
        in_specs=[hbm] * 11,
        out_specs=vmem,
        scratch_shapes=[pltpu.SMEM((6,), jnp.int32)]
        + [pltpu.VMEM(s, d) for s, d in scratch]
        + [pltpu.SemaphoreType.DMA((SEMS,))],
        compiler_params=pltpu.CompilerParams(
            collective_id=0, has_side_effects=True, vmem_limit_bytes=58 * 1024 * 1024
        ),
        name="layer",
    )(
        queries, latent_cache, lengths, slot_row, w_uv, w_o.T, resid.T, norm_gain, w_gate.T, w_up.T, w_down
    )


def solution(mesh):
    placed = (
        P("dp", "tp", None),
        P("dp", None, None),
        P("dp"),
        P(),
        P("tp", None, None),
        P("tp", "dp"),
        P(None, "dp"),
        P(),
        P("tp", "dp"),
        P("tp", "dp"),
        P("dp", "tp"),
    )
    return jax.shard_map(
        on_device, mesh=mesh, in_specs=placed, out_specs=P("dp", "tp"), check_vma=False
    )
```

time: 91.4 us -> 83 us (0.908)
  Pallas kernels: 89.9 us -> 81.5 us
    pallas_call x1, Pallas kernels: 89.9 us -> 81.5 us  [on_device(): pl.pallas_call(kernel, out_shape=jax.ShapeDtypeStruct((6, 1792), BF16), i...]
where the time goes in v3:
time: 83 us; the launch traced here: 82.9 us
  Pallas kernels  81.5 us (98%)
  local copies, waits for them, and re-layouts  1.36 us (2%)
    pallas_call x1, Pallas kernels, on_device(): pl.pallas_call(kernel, out_shape=jax.ShapeDtypeStruct((6, 1792), BF16), i...  81.5 us

profile of v3, /device:TPU:32, one launch (start us, length us, event | category | flops | bytes accessed | tf_op | source)
XLA Modules:
  0.0 82.9 jit_solution(6698286515112610699)
XLA Ops:
  0.0 81.5 %layer.1 = bf16[6,1792]{1,0:T(8,128)(2,1)} custom-call(bf16[6,32,576]{2,1,0:T(8,128)(2,1)} %q_hbm.1, bf16[6,320,576]{2,1,0:T(8,128)(2,1)} %cache_hbm.1, s32[6]{0:T(128)} %len_hbm.1, s32[384]{0:T(512)} %slot_hbm.1, bf16[32,512,128]{2,1,0:T(8,128)(2,1)} %wuv_hbm.1, bf16[112,4096]{1,0:T(8,128)(2,1)} %bitcast.6, bf16[112,384]{1,0:T(8,128)(2,1)} %bitcast.7, ...), custom_call_target="tpu_custom_call" | custom-call | tf_op jit(solution)/shard_map/layer/pallas_call | solution.py:466
  81.5 1.4 %copy.13 = bf16[6,1792]{1,0:T(8,128)(2,1)} copy(bf16[6,1792]{1,0:T(8,128)(2,1)} %layer.1) | data formatting | bytes 43008

commit v4 on v3

--- a/solution.py
+++ b/solution.py
@@ -9,7 +9,7 @@
 F32 = jnp.float32
 BF16 = jnp.bfloat16
 SCALE = 192.0 ** (-0.5)
-SEMS = 88
+SEMS = 108
 
 
 def iota(shape, axis):
@@ -37,9 +37,9 @@
     out_ref,
     len_ref, slot_ref, gain_ref, gain_s,
     q_v, cache_v, wuv_v, resid_v, w_raw, wd_v,
-    lat_s, msg_s, abuf, perm_s, z_s, wo_s, slot_s, pt_s, r_s, p_s, b_rx,
+    lat_s, msg_s, abuf, perm_s, z_s, wo_s, r_s, p_s, b_rx,
     cbuf, hid_s, x_s, w_s, sq_s, ss_s, ss_rx, gu_s, d_rx, act_s,
-    turn_s, pad_s, t_s, hid_out,
+    pt_s, pad_s, t_s, hm_s, hm_rx, hid_out,
     e1_s, e1_rx, sum_s, e2_s, e2_rx, u_s, e3_s, e3_rx,
     sems,
 ):
@@ -150,8 +150,11 @@
                 h = half * 16 + low * 2 + high
                 latent = [lat_s[j, 8 * h : 8 * h + 8, :].astype(BF16) for j in range(4)]
                 value = dot(jnp.concatenate(latent, axis=1), wuv_v[h])
-                msg_s[half, 6 * low : 6 * low + 8, 128 * high : 128 * high + 128] = value
-        abuf[half, zh, x, y] = msg_s[half, 0:48, :].astype(BF16)
+                for i in range(3):
+                    msg_s[i, half, 2 * low : 2 * low + 2, 128 * high : 128 * high + 128] = value[2 * i : 2 * i + 2]
+    for i in range(3):
+        for half in range(2):
+            abuf[i, half, zh, x, y] = msg_s[i, half].astype(BF16)
 
     pl.semaphore_wait(barrier, 19 - jnp.where(x == t, 1, 0))
 
@@ -171,15 +174,29 @@
             out.append((block(1, x, every), block(1, x, every), x_dev[k]))
         return group(out, whole)
 
-    def near(half, x_, y_):
-        return abuf.at[half, zh, x_, y_]
-
-    def far(half, x_, y_):
-        return abuf.at[half, other, x_, y_]
-
-    six, twenty_four = abuf.at[0, 0, 0:3, 0:2], abuf.at[0:2, 0, 0:3]
-    near_in = first(near, six)
-    far_in = send(abuf.at[:, zh, x, y], abuf.at[:, zh, x, y], zh_dev, abuf.at[:, other, x, y])
+    def values_at(i, z_):
+        def block(half, x_, y_):
+            return abuf.at[i, half, z_, x_, y_]
+
+        return block
+
+    def near_second(i):
+        near_in[i].wait()
+        near_in[i] = second(values_at(i, zh), abuf.at[i, 0:2, 0, 0:3])
+
+    def far_first(i):
+        far_in[i].wait()
+        far_in[i] = first(values_at(i, other), abuf.at[i, 0, 0, 0:3, 0:2])
+
+    def far_second(i):
+        far_in[i].wait()
+        far_in[i] = second(values_at(i, other), abuf.at[i, 0:2, 0, 0:3])
+
+    near_in, far_in = [], []
+    for i in range(3):
+        mine = abuf.at[i, :, zh, x, y]
+        far_in.append(send(mine, mine, zh_dev, abuf.at[i, :, other, x, y]))
+        near_in.append(first(values_at(i, zh), abuf.at[i, 0, 0, 0:3, 0:2]))
     for cp in later:
         cp.wait()
     theirs = [
@@ -190,49 +207,75 @@
         ours = ref.at[pl.ds(pl.multiple_of(at + step_ * c, step_), n)]
         other_half = ref.at[pl.ds(pl.multiple_of(at + step_ * sib, step_), n)]
         theirs.append(send(ours, ours, sib_dev, other_half))
-    row, col = iota((384, 384), 0), iota((384, 384), 1)
-    low = by(row, 48)
-    within = row - 48 * low
-    source = by(within, 6)
-    perm_s[...] = one_hot(col == source * 48 + low * 6 + (within - 6 * source))
-    near_in.wait()
-    near_in = second(near, twenty_four)
-
-    half_of = jnp.where(col >= 192, 1, 0)
-    rho = col - 192 * half_of
-    z_of = jnp.where(rho >= 96, 1, 0)
-    rho -= 96 * z_of
-    chip = by(rho, 6)
-    order = one_hot(row == ((chip * 2 + z_of) * 2 + half_of) * 6 + (rho - 6 * chip))
-    line = iota((192, 384), 0)
-    want = ((line % 64) // 2 * 2 + c) * 6 + line // 64 * 2 + line % 2
-    slots = jnp.broadcast_to(slot_ref[...][None, :], (192, 384))
-    pt_s[...] = dot(one_hot(slots == want), order).astype(BF16)
-    rows_here = one_hot(iota((192, 384), 1) == want)
-    far_in.wait()
-    far_in = first(far, six)
-
+    row, col = iota((256, 256), 0), iota((256, 256), 1)
+    perm_s[...] = one_hot(col == row % 32 // 2 * 16 + row // 32 * 2 + row % 2)
+    near_second(0)
+    near_second(1)
+    far_first(0)
+    far_first(1)
+    far_first(2)
+    near_second(2)
+
+    def slot_at(core, line):
+        chip = line % 32 // 2 * 2 + line % 64 // 32
+        return (chip * 2 + core) * 6 + line // 64 * 2 + line % 2
+
+    order_c = one_hot(iota((192, 384), 1) == slot_at(c, iota((192, 384), 0)))
+    slots = jnp.broadcast_to(slot_ref[...][None, :], (384, 384))
+    moved = dot_t(order_c, one_hot(slots == iota((384, 384), 0))).astype(BF16)
     for cp in theirs:
         cp.wait()
     r_s[...] = jnp.zeros((192, 256), F32)
     for k in range(2):
-        r_s[:, 128 * k : 128 * k + 112] = dot_t(rows_here, resid_v[k])
+        r_s[:, 128 * k : 128 * k + 112] = dot_t(moved, resid_v[k])
         wo_s[128 * k + 112 : 128 * k + 128, :] = jnp.zeros((16, 4096), BF16)
-    gain_s[...] = jnp.zeros((64, 128), F32)
-    gains = gain_ref[...].astype(F32)[None, :]
-    for j in range(64):
-        gain_s[j : j + 1, 0:112] = gains[:, 112 * j : 112 * j + 112]
-    line, row = iota((64, 64), 0), iota((64, 64), 1)
-    turn_s[...] = one_hot(row == line // 4 % 4 * 16 + line // 16 * 4 + line % 4)
-    line, row = iota((64, 48), 0), iota((64, 48), 1)
-    pad_s[...] = one_hot(
-        jnp.logical_and(line % 8 < 6, row == line % 8 // 2 * 16 + line // 8 * 2 + line % 2)
-    )
-    line, row = iota((8, 48), 0), iota((8, 48), 1)
-    t_s[...] = one_hot(jnp.logical_and(line < 6, row == line // 2 * 16 + (y * 2 + zh) * 2 + line % 2))
-    wd_v[576:640, :] = jnp.zeros((64, 1792), BF16)
-    far_in.wait()
-    far_in = second(far, twenty_four)
+    far_second(0)
+    far_second(1)
+    far_second(2)
+
+    def project(i):
+        near_in[i].wait()
+        far_in[i].wait()
+        for z_ in range(2):
+            for half in range(2):
+                placed = dot(perm_s[...], abuf[i, half, z_].reshape(256, 256)).astype(BF16)
+                for low in range(8):
+                    at = half * 2048 + low * 256
+                    z_s[32 * z_ : 32 * z_ + 32, at : at + 256] = placed[32 * low : 32 * low + 32]
+        partial = dot_t(z_s[...], wo_s[...]) + jnp.where(t == 0, r_s[64 * i : 64 * i + 64], 0.0)
+        p_s[4 * i : 4 * i + 4] = partial.astype(BF16).reshape(4, 16, 256)
+
+    b_sent, b_in = sem(), [sem() for _ in range(3)]
+    own = x == t
+
+    def deal(i):
+        for k in range(4):
+            for z_ in range(2):
+                src, dst = p_s.at[4 * i + turn(x, k)], b_rx.at[8 * i + 4 * zh + t]
+                to = dev(turn(x, k), y, lax.rem(zh + z_, 2), c, x)
+                if k + z_ > 0:
+                    remote(src, dst, b_sent, b_in[i], to).start()
+                else:
+
+                    @pl.when(jnp.logical_not(own))
+                    def _():
+                        remote(src, dst, b_sent, b_in[i], to).start()
+
+                    @pl.when(own)
+                    def _():
+                        pltpu.make_async_copy(src, dst, b_in[i]).start()
+
+    def sent():
+        for n, when in ((24, jnp.logical_not(own)), (21, own)):
+
+            @pl.when(when)
+            def _():
+                pltpu.make_async_copy(b_rx.at[0:n], b_rx.at[0:n], b_sent).wait()
+
+    tails.append(sent)
+    for i in range(3):
+        project(i)
+        deal(i)
 
     def spread(block, part, at):
         width = block.shape[1]
@@ -249,50 +292,10 @@
                 spread(w_raw[k, half, 0:256, cols].T, part, 512 * k + 256 * half)
         rest = [w_raw[k, half, 256:288, cols] for k in range(2) for half in range(2)]
         spread(jnp.concatenate(rest, axis=0).T, part, 1024)
-
-    def project(z_):
-        for half in range(2):
-            for k in range(2):
-                packed = abuf[half, z_, 2 * k : 2 * k + 2].reshape(384, 256)
-                placed = dot(perm_s[...], packed).astype(BF16)
-                for low in range(8):
-                    at = half * 2048 + low * 256
-                    z_s[48 * k : 48 * k + 48, at : at + 256] = placed[48 * low : 48 * low + 48]
-        slot_s[c, z_] = dot_t(z_s[...], wo_s[...]).astype(BF16)
-        return send(slot_s.at[c, z_], slot_s.at[c, z_], sib_dev, slot_s.at[sib, z_])
-
-    near_in.wait()
-    step = [project(zh)]
-    far_in.wait()
-    step.append(project(other))
-    for cp in step:
-        cp.wait()
-    partial = dot(pt_s[...], slot_s[...].reshape(384, 256)) + jnp.where(t == 0, r_s[...], 0.0)
-    p_s[...] = partial.astype(BF16).reshape(12, 16, 256)
-
-    b_sent, b_in = sem(), [sem() for _ in range(3)]
-    for i in range(3):
-        for k in range(4):
-            for z_ in range(2):
-                own = jnp.logical_and(jnp.logical_and(x == t, k == x), zh == z_)
-                src, dst = p_s.at[4 * i + k], b_rx.at[8 * i + 4 * zh + t]
-
-                @pl.when(jnp.logical_not(own))
-                def _():
-                    remote(src, dst, b_sent, b_in[i], dev(k, y, z_, c, x)).start()
-
-                @pl.when(own)
-                def _():
-                    pltpu.make_async_copy(src, dst, b_in[i]).start()
-
-    def sent():
-        for n, when in ((24, x != t), (21, x == t)):
-
-            @pl.when(when)
-            def _():
-                pltpu.make_async_copy(b_rx.at[0:n], b_rx.at[0:n], b_sent).wait()
-
-    tails.append(sent)
+    gain_s[...] = jnp.zeros((64, 128), F32)
+    gains = gain_ref[...].astype(F32)[None, :]
+    for j in range(64):
+        gain_s[j : j + 1, 0:112] = gains[:, 112 * j : 112 * j + 112]
 
     def blocks(i):
         def block(half, x_, y_):
@@ -300,8 +303,7 @@
 
         return block
 
-    step = []
-    for i in range(3):
+    def hidden_first(i):
         landing(b_rx.at[8 * i : 8 * i + 8], b_in[i]).wait()
         for z_ in range(2):
             at = 8 * i + 4 * z_
@@ -309,9 +311,18 @@
             for half in range(2):
                 cbuf[i, half, x, y, z_] = hidden[:, 128 * half : 128 * half + 128]
         step.append(first(blocks(i), cbuf.at[i, 0, 0:3, 0:2]))
-    for i in range(3):
+
+    def hidden_second(i):
         step[i].wait()
         step[i] = second(blocks(i), cbuf.at[i, 0:2, 0:3])
+
+    step = []
+    hidden_first(0)
+    hidden_first(1)
+    hidden_second(0)
+    hidden_first(2)
+    hidden_second(1)
+    hidden_second(2)
 
     gain = gain_s[pl.ds(pl.multiple_of(16 * t, 16), 16), :]
 
@@ -323,7 +334,9 @@
         for k in range(4):
             squares = jnp.zeros((16, 128), F32)
             for j in range(16):
-                block = cbuf[i, j % 2, k, j // 4, (j // 2) % 2].astype(F32)
+                block = cbuf[i, j % 2, k, j // 4, (j // 2) % 2]
+                hid_s[64 * i + 16 * k : 64 * i + 16 * k + 16, 128 * j : 128 * j + 128] = block
+                block = block.astype(F32)
                 squares += block * block
                 x_s[i, 16 * k : 16 * k + 16, 128 * j : 128 * j + 128] = (block * gain[j : j + 1]).astype(BF16)
             sq_s[16 * k : 16 * k + 16] = squares
@@ -350,48 +363,61 @@
         total *= lax.rsqrt(squares * (1.0 / 7168) + 1e-06)
         rest = total[:, 1024:1152]
         tail = silu(rest) * pltpu.roll(rest, 64, 1)
-        act_s[i, t, :, 0:512] = (silu(total[:, 0:512]) * total[:, 512:1024]).astype(BF16)
-        act_s[i, t, :, 512:640] = jnp.where(iota((16, 128), 1) < 64, tail, 0.0).astype(BF16)
-        mine = act_s.at[i, t]
-        return group([(mine, mine, t_dev[k]) for k in range(1, 4)], act_s.at[i, 0:3])
+        act_s[c, i, t, :, 0:512] = (silu(total[:, 0:512]) * total[:, 512:1024]).astype(BF16)
+        act_s[c, i, t, :, 512:640] = jnp.where(iota((16, 128), 1) < 64, tail, 0.0).astype(BF16)
+        mine = act_s.at[c, i, t]
+        return group([(mine, mine, t_dev[k]) for k in range(1, 4)], act_s.at[0, i, 0:3])
+
+    def share(i, copies):
+        copies.wait()
+        return send(act_s.at[c, i], act_s.at[c, i], sib_dev, act_s.at[sib, i])
 
     spots = (x, y)
     rings = (x_dev, y_dev)
 
-    def down(i, copies):
-        copies.wait()
-        rows = act_s[i].reshape(64, 640)
-        out = []
-        for half in range(2):
-            if half == 1:
-                rows = dot(turn_s[...], rows).astype(BF16)
-            part = dot(rows, wd_v[:, 896 * half : 896 * half + 896])
-            e1_s[i, half] = part.astype(BF16).reshape(4, 16, 896)
-            for k in range(1, 4):
-                out.append((e1_s.at[i, half, turn(spots[half], k)], e1_rx.at[i, half, k - 1], rings[half][k]))
-        return group(out, e1_rx.at[i])
-
-    def collect(i, copies):
-        copies.wait()
-        for half in range(2):
-            total = e1_s[i, half, spots[half]].astype(F32)
-            for k in range(3):
-                total += e1_rx[i, half, k].astype(F32)
-            sum_s[half, 16 * i : 16 * i + 16] = total.astype(BF16)
-
     wide = [gate_up(i) for i in range(3)]
-    for i in range(3):
-        for j in range(16):
-            hid_s[16 * i : 16 * i + 16, 128 * j : 128 * j + 128] = cbuf[i, j % 2, x, j // 4, (j // 2) % 2]
-    state = dot(t_s[...], hid_s[...])
+    line = iota((16, 384), 0)
+    want = jnp.where(line % 8 < 6, (place * 2 + line // 8) * 6 + line % 8, -1)
+    t_s[...] = dot_t(one_hot(slots[:16] == want), order_c).astype(BF16)
+    hm_s[...] = dot(t_s[...], hid_s[...]).reshape(2, 8, 2048)
+    hm_in = send(hm_s.at[sib], hm_rx, sib_dev, hm_rx)
+    col = iota((384, 384), 1)
+    core = jnp.where(col >= 192, 1, 0)
+    order = one_hot(iota((384, 384), 0) == slot_at(core, col - 192 * core))
+    line = iota((192, 384), 0)
+    chip = by(line, 6)
+    line -= 6 * chip
+    pt_s[0] = dot(one_hot(slots[:192] == 12 * chip + 6 * c + line), order).astype(BF16)
+    chip = (chip // 2 % 4 * 4 + chip // 8) * 2 + chip % 2
+    pt_s[1] = dot(one_hot(slots[:192] == 12 * chip + 6 * c + line), order).astype(BF16)
+    line, row = iota((64, 48), 0), iota((64, 48), 1)
+    pad_s[...] = one_hot(jnp.logical_and(line % 8 < 6, row == line // 8 * 6 + line % 8))
+    wd_v[576:640, :] = jnp.zeros((64, 1792), BF16)
+    hm_in.wait()
+    state = hm_s[c] + hm_rx[...]
     for j in range(16):
         hid_out[:, 112 * j : 112 * j + 112] = state[:, 128 * j : 128 * j + 112]
     thin = [activate(i, wide[i]) for i in range(3)]
-    ends = [down(0, thin[0]), down(1, thin[1])]
-    collect(0, ends[0])
-    ends.append(down(2, thin[2]))
-    collect(1, ends[1])
-    collect(2, ends[2])
+    ends = [share(i, thin[i]) for i in range(3)]
+    for cp in ends:
+        cp.wait()
+
+    everyone = act_s[...].reshape(384, 640)
+    step = []
+    for half in range(2):
+        rows = dot(pt_s[half], everyone).astype(BF16)
+        part = dot(rows, wd_v[:, 896 * half : 896 * half + 896])
+        e1_s[half] = part.astype(BF16).reshape(4, 48, 896)
+        parts = [
+            (e1_s.at[half, turn(spots[half], k)], e1_rx.at[half, k - 1], rings[half][k]) for k in range(1, 4)
+        ]
+        step.append(group(parts, e1_rx.at[half]))
+    for half in range(2):
+        step[half].wait()
+        total = e1_s[half, spots[half]].astype(F32)
+        for k in range(3):
+            total += e1_rx[half, k].astype(F32)
+        sum_s[half] = total.astype(BF16)
     step = []
     for half in range(2):
         e2_s[half] = dot(pad_s[...], sum_s[half]).astype(BF16).reshape(4, 16, 896)
@@ -430,18 +456,16 @@
         ((2, 2, 288, 1792), BF16),
         ((640, 1792), BF16),
         ((4, 256, 128), F32),
-        ((2, 56, 256), F32),
-        ((2, 2, 4, 4, 48, 256), BF16),
-        ((384, 384), BF16),
-        ((96, 4096), BF16),
+        ((3, 2, 16, 256), F32),
+        ((3, 2, 2, 4, 4, 16, 256), BF16),
+        ((256, 256), BF16),
+        ((64, 4096), BF16),
         ((256, 4096), BF16),
-        ((2, 2, 96, 256), BF16),
-        ((192, 384), BF16),
         ((192, 256), F32),
         ((12, 16, 256), BF16),
         ((24, 16, 256), BF16),
         ((3, 2, 4, 4, 2, 16, 128), BF16),
-        ((48, 2048), BF16),
+        ((192, 2048), BF16),
         ((3, 64, 2048), BF16),
         ((2048, 1152), BF16),
         ((64, 128), F32),
@@ -449,13 +473,15 @@
         ((3, 3, 8, 64), F32),
         ((3, 4, 16, 1152), BF16),
         ((3, 3, 16, 1152), BF16),
-        ((3, 4, 16, 640), BF16),
-        ((64, 64), BF16),
+        ((2, 3, 4, 16, 640), BF16),
+        ((2, 192, 384), BF16),
         ((64, 48), BF16),
-        ((8, 48), BF16),
+        ((16, 192), BF16),
+        ((2, 8, 2048), F32),
+        ((8, 2048), F32),
         ((8, 1792), F32),
-        ((3, 2, 4, 16, 896), BF16),
-        ((3, 2, 3, 16, 896), BF16),
+        ((2, 4, 48, 896), BF16),
+        ((2, 3, 48, 896), BF16),
         ((2, 48, 896), BF16),
         ((2, 4, 16, 896), BF16),
         ((2, 3, 16, 896), BF16),

time: 83 us -> 78.2 us (0.942); the launches traced: 82.9 us -> 76.9 us
  Pallas kernels: 81.5 us -> 75.5 us
    pallas_call x1, Pallas kernels: 81.5 us -> 75.5 us  [on_device(): pl.pallas_call(kernel, out_shape=jax.ShapeDtypeStruct((6, 1792), BF16), i...]
where the time goes in v4:
time: 78.2 us; the launch traced here: 76.9 us
  Pallas kernels  75.5 us (97%)
  local copies, waits for them, and re-layouts  1.36 us (2%)
    pallas_call x1, Pallas kernels, on_device(): pl.pallas_call(kernel, out_shape=jax.ShapeDtypeStruct((6, 1792), BF16), i...  75.5 us

profile of v4, /device:TPU:32, one launch (start us, length us, event | category | flops | bytes accessed | tf_op | source)
XLA Modules:
  0.0 76.9 jit_solution(9003363486662146645)
XLA Ops:
  0.0 75.5 %layer.1 = bf16[6,1792]{1,0:T(8,128)(2,1)} custom-call(bf16[6,32,576]{2,1,0:T(8,128)(2,1)} %q_hbm.1, bf16[6,320,576]{2,1,0:T(8,128)(2,1)} %cache_hbm.1, s32[6]{0:T(128)} %len_hbm.1, s32[384]{0:T(512)} %slot_hbm.1, bf16[32,512,128]{2,1,0:T(8,128)(2,1)} %wuv_hbm.1, bf16[112,4096]{1,0:T(8,128)(2,1)} %bitcast.6, bf16[112,384]{1,0:T(8,128)(2,1)} %bitcast.7, ...), custom_call_target="tpu_custom_call" | custom-call | tf_op jit(solution)/shard_map/layer/pallas_call | solution.py:492
  75.5 1.4 %copy.13 = bf16[6,1792]{1,0:T(8,128)(2,1)} copy(bf16[6,1792]{1,0:T(8,128)(2,1)} %layer.1) | data formatting | bytes 43008

commit v5 on v4

--- a/solution.py
+++ b/solution.py
@@ -9,7 +9,7 @@
 F32 = jnp.float32
 BF16 = jnp.bfloat16
 SCALE = 192.0 ** (-0.5)
-SEMS = 108
+SEMS = 112
 
 
 def iota(shape, axis):
@@ -35,12 +35,12 @@
 def kernel(
     q_hbm, cache_hbm, len_hbm, slot_hbm, wuv_hbm, wo_hbm, resid_hbm, gain_hbm, wg_hbm, wu_hbm, wd_hbm,
     out_ref,
-    len_ref, slot_ref, gain_ref, gain_s,
+    len_ref, slot_ref, gain_ref,
     q_v, cache_v, wuv_v, resid_v, w_raw, wd_v,
-    lat_s, msg_s, abuf, perm_s, z_s, wo_s, r_s, p_s, b_rx,
-    cbuf, hid_s, x_s, w_s, sq_s, ss_s, ss_rx, gu_s, d_rx, act_s,
-    pt_s, pad_s, t_s, hm_s, hm_rx, hid_out,
-    e1_s, e1_rx, sum_s, e2_s, e2_rx, u_s, e3_s, e3_rx,
+    lat_s, msg_s, abuf, perm_s, z_s, wo_raw, wo_s, r_s, p_s, b_rx,
+    hid, w_s, ss_s, ss_rx, gu_s, d_rx, act_s,
+    pt_s, rows_s, pad_s, t_s, hm_s, hm_rx, hid_out,
+    e1_s, e1_rx, e2_s, e2_rx, u_s, e3_s, e3_rx,
     sems,
 ):
     dp, t = lax.axis_index("dp"), lax.axis_index("tp")
@@ -105,16 +105,6 @@
     q_in = load(q_hbm, q_v)
     cache_in = load(cache_hbm, cache_v)
     wuv_in = [load(wuv_hbm.at[pl.ds(16 * i, 16)], wuv_v.at[pl.ds(16 * i, 16)]) for i in range(2)]
-    later = [
-        load(slot_hbm, slot_ref),
-        load(gain_hbm, gain_ref),
-        load(resid_hbm, resid_v.at[c]),
-        load(wo_hbm, wo_s.at[pl.ds(pl.multiple_of(128 * c, 128), 112)]),
-        load(wg_hbm, w_raw.at[0, c]),
-        load(wu_hbm, w_raw.at[1, c]),
-        load(wd_hbm.at[pl.ds(0, 256)], wd_v.at[pl.ds(pl.multiple_of(256 * c, 256), 256)]),
-        load(wd_hbm.at[pl.ds(256, 32)], wd_v.at[pl.ds(pl.multiple_of(512 + 32 * c, 32), 32)]),
-    ]
     barrier = pltpu.get_barrier_semaphore()
     for d in [sib_dev, zh_dev] + x_dev[1:] + y_dev[1:] + t_dev[1:]:
         pl.semaphore_signal(barrier, inc=1, device_id=d, device_id_type=MESH)
@@ -132,6 +122,16 @@
     len_in.wait()
     q_in.wait()
     cache_in.wait()
+    later = [
+        load(slot_hbm, slot_ref),
+        load(gain_hbm, gain_ref),
+        load(resid_hbm, resid_v.at[c]),
+        load(wo_hbm, wo_raw.at[pl.ds(pl.multiple_of(128 * c, 128), 112)]),
+        load(wg_hbm, w_raw.at[0, c]),
+        load(wu_hbm, w_raw.at[1, c]),
+        load(wd_hbm.at[pl.ds(0, 256)], wd_v.at[pl.ds(pl.multiple_of(256 * c, 256), 256)]),
+        load(wd_hbm.at[pl.ds(256, 32)], wd_v.at[pl.ds(pl.multiple_of(512 + 32 * c, 32), 32)]),
+    ]
     scores = []
     for r in range(6):
         live = iota((32, 320), 1) < len_ref[r]
@@ -203,7 +203,7 @@
         send(resid_v.at[c], resid_v.at[c], sib_dev, resid_v.at[sib]),
         send(w_raw.at[:, c], w_raw.at[:, c], sib_dev, w_raw.at[:, sib]),
     ]
-    for ref, at, step_, n in ((wo_s, 0, 128, 112), (wd_v, 0, 256, 256), (wd_v, 512, 32, 32)):
+    for ref, at, step_, n in ((wo_raw, 0, 128, 112), (wd_v, 0, 256, 256), (wd_v, 512, 32, 32)):
         ours = ref.at[pl.ds(pl.multiple_of(at + step_ * c, step_), n)]
         other_half = ref.at[pl.ds(pl.multiple_of(at + step_ * sib, step_), n)]
         theirs.append(send(ours, ours, sib_dev, other_half))
@@ -228,9 +228,32 @@
     r_s[...] = jnp.zeros((192, 256), F32)
     for k in range(2):
         r_s[:, 128 * k : 128 * k + 112] = dot_t(moved, resid_v[k])
-        wo_s[128 * k + 112 : 128 * k + 128, :] = jnp.zeros((16, 4096), BF16)
+        wo_raw[128 * k + 112 : 128 * k + 128, :] = jnp.zeros((16, 4096), BF16)
+    for k in range(8):
+        wo_s[512 * k : 512 * k + 512, :] = wo_raw[:, 512 * k : 512 * k + 512].T
     far_second(0)
+    gains = gain_ref[...].astype(F32)[None, :]
+    gains = sum(jnp.where(t == k, gains[:, 1792 * k : 1792 * k + 1792], 0.0) for k in range(4))
+
+    def spread(block, part, at):
+        block = (block.astype(F32) * gains[:, 896 * part : 896 * part + 896]).astype(BF16).T
+        for j in range(8 * part, 8 * part + 8):
+            row, src = 128 * (j % 2 * 8 + j // 2), 112 * (j - 8 * part)
+            w_s[row : row + 112, at : at + block.shape[1]] = block[src : src + 112]
+
+    def turn_weights(part):
+        cols = slice(896 * part, 896 * part + 896)
+        for k in range(2):
+            for half in range(2):
+                spread(w_raw[k, half, 0:256, cols], part, 512 * k + 256 * half)
+        rest = [w_raw[k, half, 256:288, cols] for k in range(2) for half in range(2)]
+        spread(jnp.concatenate(rest, axis=0), part, 1024)
+
+    for j in range(16):
+        w_s[128 * j + 112 : 128 * j + 128, :] = jnp.zeros((16, 1152), BF16)
+    turn_weights(0)
     far_second(1)
+    turn_weights(1)
     far_second(2)
 
     def project(i):
@@ -242,7 +265,7 @@
                 for low in range(8):
                     at = half * 2048 + low * 256
                     z_s[32 * z_ : 32 * z_ + 32, at : at + 256] = placed[32 * low : 32 * low + 32]
-        partial = dot_t(z_s[...], wo_s[...]) + jnp.where(t == 0, r_s[64 * i : 64 * i + 64], 0.0)
+        partial = dot(z_s[...], wo_s[...]) + jnp.where(t == 0, r_s[64 * i : 64 * i + 64], 0.0)
         p_s[4 * i : 4 * i + 4] = partial.astype(BF16).reshape(4, 16, 256)
 
     b_sent, b_in = sem(), [sem() for _ in range(3)]
@@ -277,44 +300,52 @@
         project(i)
         deal(i)
 
-    def spread(block, part, at):
-        width = block.shape[1]
-        for j in range(8):
-            row = 1024 * part + 128 * j
-            w_s[row : row + 112, at : at + width] = block[112 * j : 112 * j + 112]
-
-    for j in range(16):
-        w_s[128 * j + 112 : 128 * j + 128, :] = jnp.zeros((16, 1152), BF16)
-    for part in range(2):
-        cols = slice(896 * part, 896 * part + 896)
-        for k in range(2):
-            for half in range(2):
-                spread(w_raw[k, half, 0:256, cols].T, part, 512 * k + 256 * half)
-        rest = [w_raw[k, half, 256:288, cols] for k in range(2) for half in range(2)]
-        spread(jnp.concatenate(rest, axis=0).T, part, 1024)
-    gain_s[...] = jnp.zeros((64, 128), F32)
-    gains = gain_ref[...].astype(F32)[None, :]
-    for j in range(64):
-        gain_s[j : j + 1, 0:112] = gains[:, 112 * j : 112 * j + 112]
+    line = iota((16, 384), 0)
+    want = jnp.where(line % 8 < 6, (place * 2 + line // 8) * 6 + line % 8, -1)
+    t_s[...] = dot_t(one_hot(slots[:16] == want), order_c).astype(BF16)
+    col = iota((384, 384), 1)
+    core = jnp.where(col >= 192, 1, 0)
+    order = one_hot(iota((384, 384), 0) == slot_at(core, col - 192 * core))
+
+    def pieces(matrix, half):
+        for i in range(3):
+            pt_s[half, i] = jnp.concatenate(
+                [matrix[:, 192 * core + 64 * i : 192 * core + 64 * i + 64] for core in range(2)], axis=1
+            ).astype(BF16)
+
+    line = iota((192, 384), 0)
+    chip = by(line, 6)
+    line -= 6 * chip
+    pieces(dot(one_hot(slots[:192] == 12 * chip + 6 * c + line), order), 0)
+    chip = (chip // 2 % 4 * 4 + chip // 8) * 2 + chip % 2
+    pieces(dot(one_hot(slots[:192] == 12 * chip + 6 * c + line), order), 1)
+    line, row = iota((64, 48), 0), iota((64, 48), 1)
+    pad_s[...] = one_hot(jnp.logical_and(line % 8 < 6, row == line // 8 * 6 + line % 8))
+    wd_v[576:640, :] = jnp.zeros((64, 1792), BF16)
 
     def blocks(i):
         def block(half, x_, y_):
-            return cbuf.at[i, half, x_, y_]
+            rows = pl.ds(0, 64) if x_ is every else pl.ds(pl.multiple_of(16 * x_, 16), 16)
+            if y_ is every:
+                return hid.at[i, rows, pl.ds(1024 * half, 1024)]
+            return hid.at[i, rows, pl.ds(pl.multiple_of(1024 * half + 256 * y_, 256), 256)]
 
         return block
 
     def hidden_first(i):
         landing(b_rx.at[8 * i : 8 * i + 8], b_in[i]).wait()
+        rows = pl.ds(pl.multiple_of(16 * x, 16), 16)
         for z_ in range(2):
             at = 8 * i + 4 * z_
             hidden = jnp.sum(b_rx[at : at + 4].astype(F32), axis=0).astype(BF16)
             for half in range(2):
-                cbuf[i, half, x, y, z_] = hidden[:, 128 * half : 128 * half + 128]
-        step.append(first(blocks(i), cbuf.at[i, 0, 0:3, 0:2]))
+                lanes = pl.ds(pl.multiple_of(1024 * half + 256 * y + 128 * z_, 128), 128)
+                hid[i, rows, lanes] = hidden[:, 128 * half : 128 * half + 128]
+        step.append(first(blocks(i), hid.at[i, 0:16, 0:1536]))
 
     def hidden_second(i):
         step[i].wait()
-        step[i] = second(blocks(i), cbuf.at[i, 0:2, 0:3])
+        step[i] = second(blocks(i), hid.at[i, :, 0:1536])
 
     step = []
     hidden_first(0)
@@ -324,31 +355,25 @@
     hidden_second(1)
     hidden_second(2)
 
-    gain = gain_s[pl.ds(pl.multiple_of(16 * t, 16), 16), :]
-
     def silu(v):
         return v * jax.nn.sigmoid(v)
 
     def gate_up(i):
         step[i].wait()
-        for k in range(4):
-            squares = jnp.zeros((16, 128), F32)
-            for j in range(16):
-                block = cbuf[i, j % 2, k, j // 4, (j // 2) % 2]
-                hid_s[64 * i + 16 * k : 64 * i + 16 * k + 16, 128 * j : 128 * j + 128] = block
-                block = block.astype(F32)
-                squares += block * block
-                x_s[i, 16 * k : 16 * k + 16, 128 * j : 128 * j + 128] = (block * gain[j : j + 1]).astype(BF16)
-            sq_s[16 * k : 16 * k + 16] = squares
+        gu_s[i] = dot(hid[i], w_s[...]).astype(BF16).reshape(4, 16, 1152)
+        parts = [(gu_s.at[i, turn(t, k)], d_rx.at[i, k - 1], t_dev[k]) for k in range(1, 4)]
+        return [group(parts, d_rx.at[i])]
+
+    def squares_of(i):
+        squares = jnp.zeros((64, 128), F32)
+        for j in range(16):
+            block = hid[i, :, 128 * j : 128 * j + 128].astype(F32)
+            squares += block * block
         ss_s[i] = lax.dot_general(
-            jnp.ones((8, 128), F32), sq_s[...], (((1,), (1,)), ((), ())),
+            jnp.ones((8, 128), F32), squares, (((1,), (1,)), ((), ())),
             precision=lax.Precision.HIGHEST, preferred_element_type=F32,
         )
-        out = [group([(ss_s.at[i], ss_rx.at[i, k - 1], t_dev[k]) for k in range(1, 4)], ss_rx.at[i])]
-        gu_s[i] = dot(x_s[i], w_s[...]).astype(BF16).reshape(4, 16, 1152)
-        parts = [(gu_s.at[i, turn(t, k)], d_rx.at[i, k - 1], t_dev[k]) for k in range(1, 4)]
-        out.append(group(parts, d_rx.at[i]))
-        return out
+        return group([(ss_s.at[i], ss_rx.at[i, k - 1], t_dev[k]) for k in range(1, 4)], ss_rx.at[i])
 
     def activate(i, copies):
         for cp in copies:
@@ -363,80 +388,82 @@
         total *= lax.rsqrt(squares * (1.0 / 7168) + 1e-06)
         rest = total[:, 1024:1152]
         tail = silu(rest) * pltpu.roll(rest, 64, 1)
-        act_s[c, i, t, :, 0:512] = (silu(total[:, 0:512]) * total[:, 512:1024]).astype(BF16)
-        act_s[c, i, t, :, 512:640] = jnp.where(iota((16, 128), 1) < 64, tail, 0.0).astype(BF16)
-        mine = act_s.at[c, i, t]
-        return group([(mine, mine, t_dev[k]) for k in range(1, 4)], act_s.at[0, i, 0:3])
+        act_s[i, c, t, :, 0:512] = (silu(total[:, 0:512]) * total[:, 512:1024]).astype(BF16)
+        act_s[i, c, t, :, 512:640] = jnp.where(iota((16, 128), 1) < 64, tail, 0.0).astype(BF16)
+        mine = act_s.at[i, c, t]
+        return group([(mine, mine, t_dev[k]) for k in range(1, 4)], act_s.at[i, 0, 0:3])
 
     def share(i, copies):
         copies.wait()
-        return send(act_s.at[c, i], act_s.at[c, i], sib_dev, act_s.at[sib, i])
+        return send(act_s.at[i, c], act_s.at[i, c], sib_dev, act_s.at[i, sib])
 
     spots = (x, y)
     rings = (x_dev, y_dev)
 
     wide = [gate_up(i) for i in range(3)]
-    line = iota((16, 384), 0)
-    want = jnp.where(line % 8 < 6, (place * 2 + line // 8) * 6 + line % 8, -1)
-    t_s[...] = dot_t(one_hot(slots[:16] == want), order_c).astype(BF16)
-    hm_s[...] = dot(t_s[...], hid_s[...]).reshape(2, 8, 2048)
+    for i in range(3):
+        wide[i].append(squares_of(i))
+    thin = [activate(i, wide[i]) for i in range(3)]
+    hm_s[...] = dot(t_s[...], hid[...].reshape(192, 2048)).reshape(2, 8, 2048)
     hm_in = send(hm_s.at[sib], hm_rx, sib_dev, hm_rx)
-    col = iota((384, 384), 1)
-    core = jnp.where(col >= 192, 1, 0)
-    order = one_hot(iota((384, 384), 0) == slot_at(core, col - 192 * core))
-    line = iota((192, 384), 0)
-    chip = by(line, 6)
-    line -= 6 * chip
-    pt_s[0] = dot(one_hot(slots[:192] == 12 * chip + 6 * c + line), order).astype(BF16)
-    chip = (chip // 2 % 4 * 4 + chip // 8) * 2 + chip % 2
-    pt_s[1] = dot(one_hot(slots[:192] == 12 * chip + 6 * c + line), order).astype(BF16)
-    line, row = iota((64, 48), 0), iota((64, 48), 1)
-    pad_s[...] = one_hot(jnp.logical_and(line % 8 < 6, row == line // 8 * 6 + line % 8))
-    wd_v[576:640, :] = jnp.zeros((64, 1792), BF16)
+    ends = [share(i, thin[i]) for i in range(3)]
+
+    def place(half, i):
+        return dot(pt_s[half, i], act_s[i].reshape(128, 640))
+
+    for i in range(2):
+        ends[i].wait()
+        for half in range(2):
+            rows_s[half] = place(half, i) + (rows_s[half] if i else 0.0)
+    ends[2].wait()
+    cuts = (slice(0, 512), slice(512, 896))
+    rows = [(rows_s[half] + place(half, 2)).astype(BF16) for half in range(2)]
+    step = []
+    for cut in cuts:
+        for half in range(2):
+            part = dot(rows[half], wd_v[:, 896 * half + cut.start : 896 * half + cut.stop])
+            e1_s[half, :, :, cut] = part.astype(BF16).reshape(4, 48, cut.stop - cut.start)
+            parts = [
+                (e1_s.at[half, turn(spots[half], k), :, cut], e1_rx.at[half, k - 1, :, cut], rings[half][k])
+                for k in range(1, 4)
+            ]
+            step.append(group(parts, e1_rx.at[half, :, :, cut]))
     hm_in.wait()
     state = hm_s[c] + hm_rx[...]
     for j in range(16):
-        hid_out[:, 112 * j : 112 * j + 112] = state[:, 128 * j : 128 * j + 112]
-    thin = [activate(i, wide[i]) for i in range(3)]
-    ends = [share(i, thin[i]) for i in range(3)]
-    for cp in ends:
-        cp.wait()
-
-    everyone = act_s[...].reshape(384, 640)
+        at = 128 * (j % 2 * 8 + j // 2)
+        hid_out[:, 112 * j : 112 * j + 112] = state[:, at : at + 112]
+    second_step = []
+    for q, cut in enumerate(cuts):
+        parts = []
+        for half in range(2):
+            step[2 * q + half].wait()
+            total = e1_s[half, spots[half], :, cut].astype(F32)
+            for k in range(3):
+                total += e1_rx[half, k, :, cut].astype(F32)
+            padded = dot(pad_s[...], total.astype(BF16)).astype(BF16)
+            e2_s[half, :, :, cut] = padded.reshape(4, 16, cut.stop - cut.start)
+            for k in range(1, 4):
+                src = e2_s.at[half, turn(spots[1 - half], k), :, cut]
+                parts.append((src, e2_rx.at[half, k - 1, :, cut], rings[1 - half][k]))
+        second_step.append(group(parts, e2_rx.at[:, :, :, cut]))
     step = []
-    for half in range(2):
-        rows = dot(pt_s[half], everyone).astype(BF16)
-        part = dot(rows, wd_v[:, 896 * half : 896 * half + 896])
-        e1_s[half] = part.astype(BF16).reshape(4, 48, 896)
-        parts = [
-            (e1_s.at[half, turn(spots[half], k)], e1_rx.at[half, k - 1], rings[half][k]) for k in range(1, 4)
-        ]
-        step.append(group(parts, e1_rx.at[half]))
-    for half in range(2):
-        step[half].wait()
-        total = e1_s[half, spots[half]].astype(F32)
-        for k in range(3):
-            total += e1_rx[half, k].astype(F32)
-        sum_s[half] = total.astype(BF16)
-    step = []
-    for half in range(2):
-        e2_s[half] = dot(pad_s[...], sum_s[half]).astype(BF16).reshape(4, 16, 896)
-        for k in range(1, 4):
-            to = rings[1 - half][k]
-            step.append((e2_s.at[half, turn(spots[1 - half], k)], e2_rx.at[half, k - 1], to))
-    group(step, e2_rx).wait()
-    for half in range(2):
-        total = e2_s[half, spots[1 - half]].astype(F32)
-        for k in range(3):
-            total += e2_rx[half, k].astype(F32)
-        u_s[half] = total.reshape(2, 8, 896)
-    e3_s[...] = jnp.concatenate([u_s[0, other], u_s[1, other]], axis=0).astype(BF16)
-    send(e3_s, e3_rx, zh_dev, e3_rx).wait()
-    last = e3_rx[...].astype(F32)
-    for half in range(2):
-        at = 896 * half
-        total = u_s[half, zh] + last[8 * half : 8 * half + 8] + hid_out[:, at : at + 896]
-        out_ref[:, at : at + 896] = total[0:6].astype(BF16)
+    for q, cut in enumerate(cuts):
+        second_step[q].wait()
+        for half in range(2):
+            total = e2_s[half, spots[1 - half], :, cut].astype(F32)
+            for k in range(3):
+                total += e2_rx[half, k, :, cut].astype(F32)
+            u_s[half, :, :, cut] = total.reshape(2, 8, cut.stop - cut.start)
+        e3_s[:, cut] = jnp.concatenate([u_s[0, other, :, cut], u_s[1, other, :, cut]], axis=0).astype(BF16)
+        step.append(send(e3_s.at[:, cut], e3_rx.at[:, cut], zh_dev, e3_rx.at[:, cut]))
+    for q, cut in enumerate(cuts):
+        step[q].wait()
+        last = e3_rx[:, cut].astype(F32)
+        for half in range(2):
+            lanes = slice(896 * half + cut.start, 896 * half + cut.stop)
+            total = u_s[half, zh, :, cut] + last[8 * half : 8 * half + 8] + hid_out[:, lanes]
+            out_ref[:, lanes] = total[0:6].astype(BF16)
     finish()
 
 
@@ -448,7 +475,6 @@
     scratch = [
         ((384,), jnp.int32),
         ((7168,), BF16),
-        ((64, 128), F32),
         ((6, 32, 576), BF16),
         ((6, 320, 576), BF16),
         ((32, 512, 128), BF16),
@@ -461,20 +487,19 @@
         ((256, 256), BF16),
         ((64, 4096), BF16),
         ((256, 4096), BF16),
+        ((4096, 256), BF16),
         ((192, 256), F32),
         ((12, 16, 256), BF16),
         ((24, 16, 256), BF16),
-        ((3, 2, 4, 4, 2, 16, 128), BF16),
-        ((192, 2048), BF16),
         ((3, 64, 2048), BF16),
         ((2048, 1152), BF16),
-        ((64, 128), F32),
         ((3, 8, 64), F32),
         ((3, 3, 8, 64), F32),
         ((3, 4, 16, 1152), BF16),
         ((3, 3, 16, 1152), BF16),
-        ((2, 3, 4, 16, 640), BF16),
-        ((2, 192, 384), BF16),
+        ((3, 2, 4, 16, 640), BF16),
+        ((2, 3, 192, 128), BF16),
+        ((2, 192, 640), F32),
         ((64, 48), BF16),
         ((16, 192), BF16),
         ((2, 8, 2048), F32),
@@ -482,7 +507,6 @@
         ((8, 1792), F32),
         ((2, 4, 48, 896), BF16),
         ((2, 3, 48, 896), BF16),
-        ((2, 48, 896), BF16),
         ((2, 4, 16, 896), BF16),
         ((2, 3, 16, 896), BF16),
         ((2, 2, 8, 896), F32),

time: 78.2 us -> 78.3 us (level); the launches traced: 76.9 us -> 78 us
  Pallas kernels: 75.5 us -> 76.6 us
    pallas_call x1, Pallas kernels: 75.5 us -> 76.6 us  [on_device(): pl.pallas_call(kernel, out_shape=jax.ShapeDtypeStruct((6, 1792), BF16), i...]
where the time goes in v5:
time: 78.3 us; the launch traced here: 78 us
  Pallas kernels  76.6 us (98%)
  local copies, waits for them, and re-layouts  1.36 us (2%)
    pallas_call x1, Pallas kernels, on_device(): pl.pallas_call(kernel, out_shape=jax.ShapeDtypeStruct((6, 1792), BF16), i...  76.6 us

profile of v5, /device:TPU:32, one launch (start us, length us, event | category | flops | bytes accessed | tf_op | source)
XLA Modules:
  0.0 78.0 jit_solution(7015076217104994718)
XLA Ops:
  0.0 76.6 %layer.1 = bf16[6,1792]{1,0:T(8,128)(2,1)} custom-call(bf16[6,32,576]{2,1,0:T(8,128)(2,1)} %q_hbm.1, bf16[6,320,576]{2,1,0:T(8,128)(2,1)} %cache_hbm.1, s32[6]{0:T(128)} %len_hbm.1, s32[384]{0:T(512)} %slot_hbm.1, bf16[32,512,128]{2,1,0:T(8,128)(2,1)} %wuv_hbm.1, bf16[112,4096]{1,0:T(8,128)(2,1)} %bitcast.6, bf16[112,384]{1,0:T(8,128)(2,1)} %bitcast.7, ...), custom_call_target="tpu_custom_call" | custom-call | tf_op jit(solution)/shard_map/layer/pallas_call | solution.py:516
  76.6 1.4 %copy.13 = bf16[6,1792]{1,0:T(8,128)(2,1)} copy(bf16[6,1792]{1,0:T(8,128)(2,1)} %layer.1) | data formatting | bytes 43008

commit v6 on v5

--- a/solution.py
+++ b/solution.py
@@ -100,13 +100,23 @@
     x_dev = [dev(turn(x, k), y, zh, c, t) for k in range(4)]
     y_dev = [dev(x, turn(y, k), zh, c, t) for k in range(4)]
     t_dev = [(dp, turn(t, k)) for k in range(4)]
+    apart = (0, 1, 2, 1)
+    steps = sorted(
+        [(a, b) for a in range(4) for b in range(4) if a + b > 0], key=lambda s: -apart[s[0]] - apart[s[1]]
+    )
+    plane_dev = [dev(turn(x, a), turn(y, b), zh, c, t) for a, b in steps]
+    far_to_near = (
+        jnp.where(t == 0, 3, jnp.where(t == 3, 1, 2)),
+        jnp.where(t == 1, 3, jnp.where(t == 2, 1, 2)),
+        jnp.where(t < 2, 1, 3),
+    )
 
     len_in = load(len_hbm, len_ref)
     q_in = load(q_hbm, q_v)
     cache_in = load(cache_hbm, cache_v)
     wuv_in = [load(wuv_hbm.at[pl.ds(16 * i, 16)], wuv_v.at[pl.ds(16 * i, 16)]) for i in range(2)]
     barrier = pltpu.get_barrier_semaphore()
-    for d in [sib_dev, zh_dev] + x_dev[1:] + y_dev[1:] + t_dev[1:]:
+    for d in [sib_dev, zh_dev] + plane_dev + t_dev[1:]:
         pl.semaphore_signal(barrier, inc=1, device_id=d, device_id_type=MESH)
     for k in range(8):
 
@@ -156,20 +166,20 @@
         for half in range(2):
             abuf[i, half, zh, x, y] = msg_s[i, half].astype(BF16)
 
-    pl.semaphore_wait(barrier, 19 - jnp.where(x == t, 1, 0))
+    pl.semaphore_wait(barrier, 28 - jnp.where(x == t, 1, 0))
 
     every = slice(None)
 
     def first(block, whole):
         out = []
-        for k in range(1, 4):
+        for k in (2, 1, 3):
             out.append((block(0, x, y), block(0, x, y), x_dev[k]))
             out.append((block(1, x, y), block(1, x, y), y_dev[k]))
         return group(out, whole)
 
     def second(block, whole):
         out = []
-        for k in range(1, 4):
+        for k in (2, 1, 3):
             out.append((block(0, every, y), block(0, every, y), y_dev[k]))
             out.append((block(1, x, every), block(1, x, every), x_dev[k]))
         return group(out, whole)
@@ -199,14 +209,17 @@
         near_in.append(first(values_at(i, zh), abuf.at[i, 0, 0, 0:3, 0:2]))
     for cp in later:
         cp.wait()
-    theirs = [
-        send(resid_v.at[c], resid_v.at[c], sib_dev, resid_v.at[sib]),
+    def trade(ref, at, step_, n):
+        ours = ref.at[pl.ds(pl.multiple_of(at + step_ * c, step_), n)]
+        yours = ref.at[pl.ds(pl.multiple_of(at + step_ * sib, step_), n)]
+        return send(ours, ours, sib_dev, yours)
+
+    theirs = [send(resid_v.at[c], resid_v.at[c], sib_dev, resid_v.at[sib]), trade(wo_raw, 0, 128, 112)]
+    weights_in = [
         send(w_raw.at[:, c], w_raw.at[:, c], sib_dev, w_raw.at[:, sib]),
+        trade(wd_v, 0, 256, 256),
+        trade(wd_v, 512, 32, 32),
     ]
-    for ref, at, step_, n in ((wo_raw, 0, 128, 112), (wd_v, 0, 256, 256), (wd_v, 512, 32, 32)):
-        ours = ref.at[pl.ds(pl.multiple_of(at + step_ * c, step_), n)]
-        other_half = ref.at[pl.ds(pl.multiple_of(at + step_ * sib, step_), n)]
-        theirs.append(send(ours, ours, sib_dev, other_half))
     row, col = iota((256, 256), 0), iota((256, 256), 1)
     perm_s[...] = one_hot(col == row % 32 // 2 * 16 + row // 32 * 2 + row % 2)
     near_second(0)
@@ -231,30 +244,8 @@
         wo_raw[128 * k + 112 : 128 * k + 128, :] = jnp.zeros((16, 4096), BF16)
     for k in range(8):
         wo_s[512 * k : 512 * k + 512, :] = wo_raw[:, 512 * k : 512 * k + 512].T
-    far_second(0)
-    gains = gain_ref[...].astype(F32)[None, :]
-    gains = sum(jnp.where(t == k, gains[:, 1792 * k : 1792 * k + 1792], 0.0) for k in range(4))
-
-    def spread(block, part, at):
-        block = (block.astype(F32) * gains[:, 896 * part : 896 * part + 896]).astype(BF16).T
-        for j in range(8 * part, 8 * part + 8):
-            row, src = 128 * (j % 2 * 8 + j // 2), 112 * (j - 8 * part)
-            w_s[row : row + 112, at : at + block.shape[1]] = block[src : src + 112]
-
-    def turn_weights(part):
-        cols = slice(896 * part, 896 * part + 896)
-        for k in range(2):
-            for half in range(2):
-                spread(w_raw[k, half, 0:256, cols], part, 512 * k + 256 * half)
-        rest = [w_raw[k, half, 256:288, cols] for k in range(2) for half in range(2)]
-        spread(jnp.concatenate(rest, axis=0), part, 1024)
-
-    for j in range(16):
-        w_s[128 * j + 112 : 128 * j + 128, :] = jnp.zeros((16, 1152), BF16)
-    turn_weights(0)
-    far_second(1)
-    turn_weights(1)
-    far_second(2)
+    for i in range(3):
+        far_second(i)
 
     def project(i):
         near_in[i].wait()
@@ -272,8 +263,8 @@
     own = x == t
 
     def deal(i):
-        for k in range(4):
-            for z_ in range(2):
+        for z_ in (1, 0):
+            for k in (2, 1, 3, 0):
                 src, dst = p_s.at[4 * i + turn(x, k)], b_rx.at[8 * i + 4 * zh + t]
                 to = dev(turn(x, k), y, lax.rem(zh + z_, 2), c, x)
                 if k + z_ > 0:
@@ -300,37 +291,30 @@
         project(i)
         deal(i)
 
-    line = iota((16, 384), 0)
-    want = jnp.where(line % 8 < 6, (place * 2 + line // 8) * 6 + line % 8, -1)
-    t_s[...] = dot_t(one_hot(slots[:16] == want), order_c).astype(BF16)
-    col = iota((384, 384), 1)
-    core = jnp.where(col >= 192, 1, 0)
-    order = one_hot(iota((384, 384), 0) == slot_at(core, col - 192 * core))
-
-    def pieces(matrix, half):
-        for i in range(3):
-            pt_s[half, i] = jnp.concatenate(
-                [matrix[:, 192 * core + 64 * i : 192 * core + 64 * i + 64] for core in range(2)], axis=1
-            ).astype(BF16)
-
-    line = iota((192, 384), 0)
-    chip = by(line, 6)
-    line -= 6 * chip
-    pieces(dot(one_hot(slots[:192] == 12 * chip + 6 * c + line), order), 0)
-    chip = (chip // 2 % 4 * 4 + chip // 8) * 2 + chip % 2
-    pieces(dot(one_hot(slots[:192] == 12 * chip + 6 * c + line), order), 1)
-    line, row = iota((64, 48), 0), iota((64, 48), 1)
-    pad_s[...] = one_hot(jnp.logical_and(line % 8 < 6, row == line // 8 * 6 + line % 8))
-    wd_v[576:640, :] = jnp.zeros((64, 1792), BF16)
-
-    def blocks(i):
-        def block(half, x_, y_):
-            rows = pl.ds(0, 64) if x_ is every else pl.ds(pl.multiple_of(16 * x_, 16), 16)
-            if y_ is every:
-                return hid.at[i, rows, pl.ds(1024 * half, 1024)]
-            return hid.at[i, rows, pl.ds(pl.multiple_of(1024 * half + 256 * y_, 256), 256)]
-
-        return block
+
+    for cp in weights_in:
+        cp.wait()
+    gains = gain_ref[...].astype(F32)[None, :]
+    gains = sum(jnp.where(t == k, gains[:, 1792 * k : 1792 * k + 1792], 0.0) for k in range(4))
+
+    def spread(block, part, at):
+        block = (block.astype(F32) * gains[:, 896 * part : 896 * part + 896]).astype(BF16).T
+        for j in range(8 * part, 8 * part + 8):
+            row, src = 128 * (j // 4 * 4 + j % 2 * 2 + j // 2 % 2), 112 * (j - 8 * part)
+            w_s[row : row + 112, at : at + block.shape[1]] = block[src : src + 112]
+
+    def turn_weights(part):
+        cols = slice(896 * part, 896 * part + 896)
+        for k in range(2):
+            for half in range(2):
+                spread(w_raw[k, half, 0:256, cols], part, 512 * k + 256 * half)
+        rest = [w_raw[k, half, 256:288, cols] for k in range(2) for half in range(2)]
+        spread(jnp.concatenate(rest, axis=0), part, 1024)
+
+    for j in range(16):
+        w_s[128 * j + 112 : 128 * j + 128, :] = jnp.zeros((16, 1152), BF16)
+    turn_weights(0)
+    turn_weights(1)
 
     def hidden_first(i):
         landing(b_rx.at[8 * i : 8 * i + 8], b_in[i]).wait()
@@ -339,21 +323,14 @@
             at = 8 * i + 4 * z_
             hidden = jnp.sum(b_rx[at : at + 4].astype(F32), axis=0).astype(BF16)
             for half in range(2):
-                lanes = pl.ds(pl.multiple_of(1024 * half + 256 * y + 128 * z_, 128), 128)
+                lanes = pl.ds(pl.multiple_of(512 * y + 256 * half + 128 * z_, 128), 128)
                 hid[i, rows, lanes] = hidden[:, 128 * half : 128 * half + 128]
-        step.append(first(blocks(i), hid.at[i, 0:16, 0:1536]))
-
-    def hidden_second(i):
-        step[i].wait()
-        step[i] = second(blocks(i), hid.at[i, :, 0:1536])
+        mine = hid.at[i, rows, pl.ds(pl.multiple_of(512 * y, 512), 512)]
+        step.append(group([(mine, mine, d) for d in plane_dev], z_s.at[0:48, 0:2560]))
 
     step = []
-    hidden_first(0)
-    hidden_first(1)
-    hidden_second(0)
-    hidden_first(2)
-    hidden_second(1)
-    hidden_second(2)
+    for i in range(3):
+        hidden_first(i)
 
     def silu(v):
         return v * jax.nn.sigmoid(v)
@@ -361,7 +338,7 @@
     def gate_up(i):
         step[i].wait()
         gu_s[i] = dot(hid[i], w_s[...]).astype(BF16).reshape(4, 16, 1152)
-        parts = [(gu_s.at[i, turn(t, k)], d_rx.at[i, k - 1], t_dev[k]) for k in range(1, 4)]
+        parts = [(gu_s.at[i, turn(t, k)], d_rx.at[i, k - 1], (dp, turn(t, k))) for k in far_to_near]
         return [group(parts, d_rx.at[i])]
 
     def squares_of(i):
@@ -391,7 +368,7 @@
         act_s[i, c, t, :, 0:512] = (silu(total[:, 0:512]) * total[:, 512:1024]).astype(BF16)
         act_s[i, c, t, :, 512:640] = jnp.where(iota((16, 128), 1) < 64, tail, 0.0).astype(BF16)
         mine = act_s.at[i, c, t]
-        return group([(mine, mine, t_dev[k]) for k in range(1, 4)], act_s.at[i, 0, 0:3])
+        return group([(mine, mine, (dp, turn(t, k))) for k in far_to_near], act_s.at[i, 0, 0:3])
 
     def share(i, copies):
         copies.wait()
@@ -403,6 +380,28 @@
     wide = [gate_up(i) for i in range(3)]
     for i in range(3):
         wide[i].append(squares_of(i))
+    line = iota((16, 384), 0)
+    want = jnp.where(line % 8 < 6, (place * 2 + line // 8) * 6 + line % 8, -1)
+    t_s[...] = dot_t(one_hot(slots[:16] == want), order_c).astype(BF16)
+    col = iota((384, 384), 1)
+    core = jnp.where(col >= 192, 1, 0)
+    order = one_hot(iota((384, 384), 0) == slot_at(core, col - 192 * core))
+
+    def pieces(matrix, half):
+        for i in range(3):
+            pt_s[half, i] = jnp.concatenate(
+                [matrix[:, 192 * core + 64 * i : 192 * core + 64 * i + 64] for core in range(2)], axis=1
+            ).astype(BF16)
+
+    line = iota((192, 384), 0)
+    chip = by(line, 6)
+    line -= 6 * chip
+    pieces(dot(one_hot(slots[:192] == 12 * chip + 6 * c + line), order), 0)
+    chip = (chip // 2 % 4 * 4 + chip // 8) * 2 + chip % 2
+    pieces(dot(one_hot(slots[:192] == 12 * chip + 6 * c + line), order), 1)
+    line, row = iota((64, 48), 0), iota((64, 48), 1)
+    pad_s[...] = one_hot(jnp.logical_and(line % 8 < 6, row == line // 8 * 6 + line % 8))
+    wd_v[576:640, :] = jnp.zeros((64, 1792), BF16)
     thin = [activate(i, wide[i]) for i in range(3)]
     hm_s[...] = dot(t_s[...], hid[...].reshape(192, 2048)).reshape(2, 8, 2048)
     hm_in = send(hm_s.at[sib], hm_rx, sib_dev, hm_rx)
@@ -425,13 +424,13 @@
             e1_s[half, :, :, cut] = part.astype(BF16).reshape(4, 48, cut.stop - cut.start)
             parts = [
                 (e1_s.at[half, turn(spots[half], k), :, cut], e1_rx.at[half, k - 1, :, cut], rings[half][k])
-                for k in range(1, 4)
+                for k in (2, 1, 3)
             ]
             step.append(group(parts, e1_rx.at[half, :, :, cut]))
     hm_in.wait()
     state = hm_s[c] + hm_rx[...]
     for j in range(16):
-        at = 128 * (j % 2 * 8 + j // 2)
+        at = 128 * (j // 4 * 4 + j % 2 * 2 + j // 2 % 2)
         hid_out[:, 112 * j : 112 * j + 112] = state[:, at : at + 112]
     second_step = []
     for q, cut in enumerate(cuts):
@@ -443,7 +442,7 @@
                 total += e1_rx[half, k, :, cut].astype(F32)
             padded = dot(pad_s[...], total.astype(BF16)).astype(BF16)
             e2_s[half, :, :, cut] = padded.reshape(4, 16, cut.stop - cut.start)
-            for k in range(1, 4):
+            for k in (2, 1, 3):
                 src = e2_s.at[half, turn(spots[1 - half], k), :, cut]
                 parts.append((src, e2_rx.at[half, k - 1, :, cut], rings[1 - half][k]))
         second_step.append(group(parts, e2_rx.at[:, :, :, cut]))

time: 78.3 us -> 76.6 us (0.978); the launches traced: 78 us -> 75.5 us
  Pallas kernels: 76.6 us -> 74.1 us
    pallas_call x1, Pallas kernels: 76.6 us -> 74.1 us  [on_device(): pl.pallas_call(kernel, out_shape=jax.ShapeDtypeStruct((6, 1792), BF16), i...]
where the time goes in v6:
time: 76.6 us; the launch traced here: 75.5 us
  Pallas kernels  74.1 us (97%)
  local copies, waits for them, and re-layouts  1.36 us (2%)
    pallas_call x1, Pallas kernels, on_device(): pl.pallas_call(kernel, out_shape=jax.ShapeDtypeStruct((6, 1792), BF16), i...  74.1 us

profile of v6, /device:TPU:32, one launch (start us, length us, event | category | flops | bytes accessed | tf_op | source)
XLA Modules:
  0.0 75.5 jit_solution(9131003933428308871)
XLA Ops:
  0.0 74.1 %layer.1 = bf16[6,1792]{1,0:T(8,128)(2,1)} custom-call(bf16[6,32,576]{2,1,0:T(8,128)(2,1)} %q_hbm.1, bf16[6,320,576]{2,1,0:T(8,128)(2,1)} %cache_hbm.1, s32[6]{0:T(128)} %len_hbm.1, s32[384]{0:T(512)} %slot_hbm.1, bf16[32,512,128]{2,1,0:T(8,128)(2,1)} %wuv_hbm.1, bf16[112,4096]{1,0:T(8,128)(2,1)} %bitcast.6, bf16[112,384]{1,0:T(8,128)(2,1)} %bitcast.7, ...), custom_call_target="tpu_custom_call" | custom-call | tf_op jit(solution)/shard_map/layer/pallas_call | solution.py:515
  74.1 1.4 %copy.13 = bf16[6,1792]{1,0:T(8,128)(2,1)} copy(bf16[6,1792]{1,0:T(8,128)(2,1)} %layer.1) | data formatting | bytes 43008

commit v7 on v6

--- a/solution.py
+++ b/solution.py
@@ -9,7 +9,7 @@
 F32 = jnp.float32
 BF16 = jnp.bfloat16
 SCALE = 192.0 ** (-0.5)
-SEMS = 112
+SEMS = 101
 
 
 def iota(shape, axis):
@@ -350,7 +350,6 @@
             jnp.ones((8, 128), F32), squares, (((1,), (1,)), ((), ())),
             precision=lax.Precision.HIGHEST, preferred_element_type=F32,
         )
-        return group([(ss_s.at[i], ss_rx.at[i, k - 1], t_dev[k]) for k in range(1, 4)], ss_rx.at[i])
 
     def activate(i, copies):
         for cp in copies:
@@ -359,7 +358,7 @@
         squares = ss_s[i]
         for k in range(3):
             total += d_rx[i, k].astype(F32)
-            squares += ss_rx[i, k]
+            squares += ss_rx[k, i]
         here = iota((16, 64), 1) == 16 * t + iota((16, 64), 0)
         squares = jnp.sum(jnp.where(here, squares[0:1], 0.0), axis=1, keepdims=True)
         total *= lax.rsqrt(squares * (1.0 / 7168) + 1e-06)
@@ -379,7 +378,8 @@
 
     wide = [gate_up(i) for i in range(3)]
     for i in range(3):
-        wide[i].append(squares_of(i))
+        squares_of(i)
+    wide[0].append(group([(ss_s, ss_rx.at[k - 1], t_dev[k]) for k in range(1, 4)], ss_rx))
     line = iota((16, 384), 0)
     want = jnp.where(line % 8 < 6, (place * 2 + line // 8) * 6 + line % 8, -1)
     t_s[...] = dot_t(one_hot(slots[:16] == want), order_c).astype(BF16)

time: 76.6 us -> 76.7 us (level)
  no operation moved by 1% of the time
where the time goes in v7:
time: 76.7 us; the launch traced here: 75.6 us
  Pallas kernels  74.3 us (97%)
  local copies, waits for them, and re-layouts  1.36 us (2%)
    pallas_call x1, Pallas kernels, on_device(): pl.pallas_call(kernel, out_shape=jax.ShapeDtypeStruct((6, 1792), BF16), i...  74.3 us

profile of v7, /device:TPU:32, one launch (start us, length us, event | category | flops | bytes accessed | tf_op | source)
XLA Modules:
  0.0 75.6 jit_solution(17917890993484639340)
XLA Ops:
  0.0 74.3 %layer.1 = bf16[6,1792]{1,0:T(8,128)(2,1)} custom-call(bf16[6,32,576]{2,1,0:T(8,128)(2,1)} %q_hbm.1, bf16[6,320,576]{2,1,0:T(8,128)(2,1)} %cache_hbm.1, s32[6]{0:T(128)} %len_hbm.1, s32[384]{0:T(512)} %slot_hbm.1, bf16[32,512,128]{2,1,0:T(8,128)(2,1)} %wuv_hbm.1, bf16[112,4096]{1,0:T(8,128)(2,1)} %bitcast.6, bf16[112,384]{1,0:T(8,128)(2,1)} %bitcast.7, ...), custom_call_target="tpu_custom_call" | custom-call | tf_op jit(solution)/shard_map/layer/pallas_call | solution.py:515
  74.3 1.4 %copy.13 = bf16[6,1792]{1,0:T(8,128)(2,1)} copy(bf16[6,1792]{1,0:T(8,128)(2,1)} %layer.1) | data formatting | bytes 43008
